TPU v7x, 256 devices: a whole 4x4x8 slice. The times are simulated.
256 devices in a mesh: docs: 32 (over y, x, core), grp: 8 (over z).
Axes of the slice: x: 4, y: 4, z: 8, core: 2. Of those that a mesh axis runs over, the one named last changes fastest.
Arguments:
- embeds: bfloat16 [65536, 1024], P('docs'), may hold values from -300 to 300
- cluster_of: int32 [65536], P('docs'), may hold values from 0 to 31, as said below
Outputs:
- nearest: float32 [65536], P('docs')
Inputs may be any that keep to these rules, and one draw needn't show every extreme that they name: `cluster_of`: each document names one cluster. The 2048 documents of one docs shard name no cluster more than 128 times and some cluster exactly 128 times; every cluster is named by 128 or more documents.
All inputs are finite; a program needn't handle non-finite values.
Results may differ from a plain program's by a relative error of at most 0.0005.
Values may be sent and summed in bfloat16 or wider, within the bound.
A program may use at most 64 MiB of HBM per device.

v0:
```python
import jax
import jax.numpy as jnp
from jax import lax
from jax.sharding import PartitionSpec as P

EPSILON = 1e-06
LOWEST = -3e38


def normalize(embeds):
    values = embeds.astype(jnp.float32)
    inverse = lax.rsqrt(jnp.sum(values * values, axis=1, keepdims=True) + EPSILON)
    return (values * inverse).astype(jnp.bfloat16)


def cluster_rank(cluster_of, cluster_count):
    onehot = (cluster_of[:, None] == jnp.arange(cluster_count, dtype=jnp.int32)[None, :]).astype(
        jnp.int32
    )
    earlier = jnp.cumsum(onehot, axis=0) - onehot
    return jnp.sum(earlier * onehot, axis=1)


def masked_scores(left_rows, right_rows, left_start, left_valid, right_valid):
    similarity = lax.dot_general(
        left_rows, right_rows, (((1,), (1,)), ((), ())), preferred_element_type=jnp.float32
    )
    left_index = left_start + jnp.arange(left_rows.shape[0], dtype=jnp.int32)
    right_index = jnp.arange(right_rows.shape[0], dtype=jnp.int32)
    allowed = (
        left_valid[:, None] & right_valid[None, :] & (left_index[:, None] != right_index[None, :])
    )
    return jnp.where(allowed, similarity, LOWEST)


def local(embeds, cluster_of):
    shard_rows = embeds.shape[0]
    feature_count = embeds.shape[1]
    doc_groups = lax.axis_size("docs")
    group_size = lax.axis_size("grp")
    slot_count = 2 * shard_rows // doc_groups
    capacity = doc_groups * slot_count
    unit_rows = normalize(embeds)
    member_rank = cluster_rank(cluster_of, doc_groups)
    position = cluster_of * slot_count + member_rank
    outgoing = jnp.zeros((capacity, feature_count), jnp.bfloat16).at[position].set(unit_rows)
    outgoing = outgoing.reshape(doc_groups, slot_count, feature_count)
    present = (
        jnp.zeros((capacity,), jnp.bfloat16).at[position].set(jnp.ones((shard_rows,), jnp.bfloat16))
    )
    present = present.reshape(doc_groups, slot_count)
    my_group = lax.axis_index("grp")
    members, member_flags = (
        lax.all_to_all(outgoing, "docs", split_axis=0, concat_axis=0, tiled=True),
        lax.all_to_all(present, "docs", split_axis=0, concat_axis=0, tiled=True),
    )
    members = members.reshape(capacity, feature_count)
    member_valid = member_flags.reshape(capacity) > 0
    empty = jnp.full((capacity,), LOWEST, jnp.float32)
    share_rows = capacity // group_size
    row_start = my_group * share_rows
    own_rows = lax.dynamic_slice_in_dim(members, row_start, share_rows, 0)
    own_valid = lax.dynamic_slice_in_dim(member_valid, row_start, share_rows, 0)
    scores = masked_scores(own_rows, members, row_start, own_valid, member_valid)
    row_best = jnp.max(scores, axis=1)
    nearest_slot = lax.dynamic_update_slice_in_dim(empty, row_best, row_start, 0)
    nearest_slot = lax.pmax(nearest_slot, "grp")
    returned = lax.all_to_all(
        nearest_slot.reshape(doc_groups, slot_count),
        "docs",
        split_axis=0,
        concat_axis=0,
        tiled=True,
    )
    return returned.reshape(-1)[position]


def solution(mesh):
    return jax.shard_map(
        local,
        mesh=mesh,
        in_specs=(P("docs", None), P("docs")),
        out_specs=P("docs"),
        check_vma=False,
    )
```

profile of v0, /device:TPU:1, one launch (start us, length us, event | category | flops | bytes accessed | tf_op | source)
XLA Modules:
  0.0 240.7 jit_solution(7421554604466299881)
XLA Ops:
  0.0 0.7 fusion.11
  0.7 9.1 %reduce-window.6 = s32[32,16,128]{2,1,0:T(8,128)S(1)} reduce-window(s32[32,16,128]{2,1,0:T(8,128)S(1)} %fusion.11, s32[]{:T(128)} %constant.14.clone.1), window={size=1x1x128 pad=0_0x0_0x127_0}, to_apply=%region_0.0 | reduce-window | flops 8323072 | bytes 524292 | tf_op jit(solution)/shard_map/reduce-window
  9.8 0.1 slice.10
  9.9 0.2 copy.9
  10.2 0.2 reduce-window.9
  10.4 0.1 broadcast_add_fusion
  10.5 0.8 fusion.10
  11.3 0.7 broadcast_clamp_fusion
  12.1 14.6 %scatter_custom_fusion = bf16[4096]{0:T(1024)(128)(2,1)S(1)} fusion(s32[2048]{0:T(1024)S(1)} %get-tuple-element.6, bf16[2048]{0:T(1024)(128)(2,1)S(1)} %broadcast.48, bf16[]{:T(256)} %constant.12.clone.1), kind=kCustom, calls=%fused_computation.26 | custom fusion | bytes 8194 | tf_op jit(solution)/shard_map/scatter | solution.py:49
  26.6 0.6 copy.7
  27.3 8.6 %all-to-all-start = ((bf16[32,1,128]{2,1,0:T(2,128)(2,1)}), bf16[32,1,128]{2,1,0:T(2,128)(2,1)S(1)}, u32[]{:S(2)}, u32[]{:S(2)}) async-start(bf16[32,1,128]{2,1,0:T(2,128)(2,1)} %copy.7), calls=%async_computation | async-start | bytes 32768 | tf_op jit(solution)/shard_map/all_to_all | solution.py:55
  35.8 3.1 %fusion = f32[2048]{0:T(1024)S(1)} fusion(bf16[2048,1024]{1,0:T(8,128)(2,1)} %param.2), kind=kLoop, calls=%fused_computation.5 | loop fusion | flops 6289408 | bytes 4202496 | tf_op jit(solution)/shard_map/reduce_sum | solution.py:12
  38.9 15.8 %scatter_custom_fusion.1 = bf16[4096,1024]{1,0:T(8,128)(2,1)} fusion(s32[2048]{0:T(1024)S(1)} %get-tuple-element.6, bf16[2048,1024]{1,0:T(8,128)(2,1)} %param.2, f32[2048]{0:T(1024)S(1)} %add_rsqrt_fusion, bf16[]{:T(256)} %constant.12.clone.1), kind=kCustom, calls=%fused_computation.10 | custom fusion | flops 6291456 | bytes 12591106 | tf_op jit(solution)/shard_map/scatter | solution.py:46
  54.7 0.0 all-to-all-done
  54.7 7.4 %all-to-all-start.1 = ((bf16[32,128,1024]{2,1,0:T(8,128)(2,1)}), bf16[32,128,1024]{2,1,0:T(8,128)(2,1)}, u32[]{:S(2)}, u32[]{:S(2)}) async-start(bf16[32,128,1024]{2,1,0:T(8,128)(2,1)} %bitcast.30), calls=%async_computation.1 | async-start | bytes 16777216 | tf_op jit(solution)/shard_map/all_to_all | solution.py:54
  62.2 0.1 dynamic_slice.6
  62.3 99.6 %all-to-all-done.1 = bf16[32,128,1024]{2,1,0:T(8,128)(2,1)} async-done(((bf16[32,128,1024]{2,1,0:T(8,128)(2,1)}), bf16[32,128,1024]{2,1,0:T(8,128)(2,1)}, u32[]{:S(2)}, u32[]{:S(2)}) %all-to-all-start.1) | async-done | bytes 8388640 | tf_op jit(solution)/shard_map/all_to_all | solution.py:54
  161.9 9.1 %select_reduce_fusion = f32[512]{0:T(512)S(1)} fusion(bf16[4096,1024]{1,0:T(8,128)(2,1)} %bitcast.7, s32[512]{0:T(512)S(1)} %iota_add_fusion, pred[4096]{0:T(1024)(128)(4,1)S(1)} %compare_bitcast_fusion, pred[512]{0:T(512)(128)(4,1)S(1)} %dynamic_slice.6, s32[]{:T(128)S(6)} %select_n.15), kind=kOutput, calls=%fused_computation.7 | convolution fusion | flops 4305452544 | bytes 9445892 | tf_op jit(solution)/shard_map/dot_general | solution.py:25
  171.0 0.3 dynamic_update_slice.3
  171.3 25.5 %pmax.7 = f32[32,1,128]{2,1,0:T(1,128)S(1)} all-reduce(f32[32,1,128]{2,1,0:T(1,128)S(1)} %bitcast.35), channel_id=1, replica_groups=mesh['docs'=32,'grp'=8] {'grp'}, use_global_device_ids=true, to_apply=%region_7.8 | all-reduce | flops 4096 | bytes 32768 | tf_op jit(solution)/shard_map/pmax | solution.py:67
  196.8 23.3 %all_to_all.23 = f32[32,1,128]{2,1,0:T(1,128)S(1)} all-to-all(f32[32,1,128]{2,1,0:T(1,128)S(1)} %pmax.7), channel_id=1, replica_groups=mesh['docs'=32,'grp'=8] {'docs'}, dimensions={0} | all-to-all | bytes 32768 | tf_op jit(solution)/shard_map/all_to_all | solution.py:68
  220.1 20.5 %gather_fusion = f32[2048]{0:T(1024)} fusion(f32[4096]{0:T(1024)S(1)} %bitcast.29, s32[2048]{0:T(1024)S(1)} %get-tuple-element.5), kind=kCustom, calls=%fused_computation | custom fusion | bytes 24576 | tf_op jit(solution)/shard_map/gather | solution.py:75
  (5 shorter events, 0.0 us)
Async XLA Ops:
  27.3 27.5 %all-to-all-start = ((bf16[32,1,128]{2,1,0:T(2,128)(2,1)}), bf16[32,1,128]{2,1,0:T(2,128)(2,1)S(1)}, u32[]{:S(2)}, u32[]{:S(2)}) async-start(bf16[32,1,128]{2,1,0:T(2,128)(2,1)} %copy.7), calls=%async_computation | async-start | bytes 32768 | tf_op jit(solution)/shard_map/all_to_all | solution.py:55
  54.7 107.2 %all-to-all-start.1 = ((bf16[32,128,1024]{2,1,0:T(8,128)(2,1)}), bf16[32,128,1024]{2,1,0:T(8,128)(2,1)}, u32[]{:S(2)}, u32[]{:S(2)}) async-start(bf16[32,128,1024]{2,1,0:T(8,128)(2,1)} %bitcast.30), calls=%async_computation.1 | async-start | bytes 16777216 | tf_op jit(solution)/shard_map/all_to_all | solution.py:54
where the time goes:
time: 241 us
  waiting for transfers between devices  99.6 us (41%)
  blocking collectives  48.8 us (20%)
  local copies, waits for them, and re-layouts  36.5 us (15%)
  other arithmetic  30.6 us (13%)
  starting transfers between devices  16 us (7%)
  matrix products  9.1 us (4%)
    all_to_all x1, waiting for transfers between devices, local(): lax.all_to_all(outgoing, 'docs', split_axis=0, concat_axis=0, tiled=True)  99.6 us
    pmax x1, blocking collectives, local(): nearest_slot = lax.pmax(nearest_slot, 'grp')  25.5 us
    all_to_all x1, blocking collectives, local(): lax.all_to_all(nearest_slot.reshape(doc_groups, slot_count), 'docs', spli...  23.3 us
    gather x1, local copies, waits for them, and re-layouts, local(): return returned.reshape(-1)[position]  20.5 us
    scatter x1, other arithmetic, local(): jnp.zeros((capacity, feature_count), jnp.bfloat16).at[position]  15.8 us
    scatter x1, local copies, waits for them, and re-layouts, local(): jnp.zeros((capacity,), jnp.bfloat16).at[position]  14.6 us
    another operation x3, other arithmetic  9.41 us
    dot_general x1, matrix products, masked_scores(): lax.dot_general(left_rows, right_rows, (((1,), (1,)), ((), ())), preferre...  9.1 us
  transfers between devices with their start and end apart: 2, of which 1 were waited for; matrix products, arithmetic and copies ran while one was open for 8% of the time, Pallas kernels for 0%

commit v1 on v0

v1 whole, which is shorter than its diff:
```python
import jax
import jax.numpy as jnp
from jax import lax
from jax.experimental import pallas as pl
from jax.experimental.pallas import tpu as pltpu
from jax.sharding import PartitionSpec as P


EPSILON = 1e-06
LOWEST = -3e38
FAR = -1e30
PADDED = 2.0

SIDE = 4
PLANES = 8
DOCS = 2048
WIDTH = 1024
SLOTS = 128
STAGES = 4
PIECE = SLOTS // STAGES
SOURCES = 16
HALF = SOURCES * PIECE
STAGE_ROWS = 2 * HALF
MEMBERS = STAGES * STAGE_ROWS
COLS = 256
LINES = DOCS // 128

MESH = pl.DeviceIdType.MESH
F32 = jnp.float32
BF16 = jnp.bfloat16
NT = (((1,), (1,)), ((), ()))


def iota(shape, axis):
    return lax.broadcasted_iota(jnp.int32, shape, axis)


def kernel(
    cluster_ref, embeds_ref, out_ref,
    rows, pick, gathered, blocks, relay, members, row_bias, col_bias, row_max, col_max, row_best, answer,
    returned, partial, lane_of, line_of,
    load_sem, sent, relay_arrive, forwarded, arrive, swap_sent, swap_arrive, back_sent, back_arrive,
    part_sent, part_arrive,
):
    docs = lax.axis_index("docs")
    z = lax.axis_index("grp")
    core = lax.rem(docs, 2)
    x = lax.rem(lax.div(docs, 2), SIDE)
    y = lax.div(docs, 2 * SIDE)
    role = lax.rem(x - y + z + SIDE, SIDE)
    sibling = docs + 1 - 2 * core
    v = lax.rem(y - z + PLANES, SIDE)

    def place(px, py, pcore):
        return (lax.rem(py, SIDE) * SIDE + lax.rem(px, SIDE)) * 2 + pcore

    def plane(pz):
        return lax.rem(pz + PLANES, PLANES)

    target = [place(v, y, core), place(v + 3, y + 3, core), place(v + 1, y + 2, core), place(v + 2, y + 1, core)]
    home = [z, z, plane(z + 1), plane(z - 1)]
    number = [SIDE * home[b] + lax.rem(y + SIDE - b, SIDE) for b in range(4)]
    column = [role, lax.rem(role + 1, SIDE), lax.rem(role + 3, SIDE), lax.rem(role + 2, SIDE)]

    load = pltpu.make_async_copy(embeds_ref, rows, load_sem)
    load.start()

    barrier = pltpu.get_barrier_semaphore()

    def greet(device):
        pl.semaphore_signal(barrier, inc=1, device_id=device, device_id_type=MESH)

    greet((sibling, z))
    for step in range(1, PLANES):
        greet((docs, plane(z + step)))

    @pl.when(role == 0)
    def _():
        for dx in range(1, SIDE):
            greet((place(x + dx, y, core), z))
        for dx in range(SIDE):
            greet((place(x + dx, y + 1, core), z))

    @pl.when((role == 3) | (role == 1))
    def _():
        for dx in range(SIDE):
            greet((place(x + dx, y + 2 + lax.div(3 - role, 2), core), z))

    clusters = cluster_ref[...]
    member = [jnp.where(clusters == number[b], 1.0, 0.0).astype(F32) for b in range(4)]
    stacked = jnp.concatenate(member, axis=0).astype(BF16)
    before = jnp.where(iota((128, 128), 0) < iota((128, 128), 1), 1.0, 0.0).astype(BF16)
    within = jnp.dot(stacked, before, preferred_element_type=F32)
    totals = jnp.dot(stacked, jnp.ones((128, 128), BF16), preferred_element_type=F32)
    lines = 4 * LINES
    above = (iota((lines, lines), 1) < iota((lines, lines), 0)) & (
        lax.div(iota((lines, lines), 1), LINES) == lax.div(iota((lines, lines), 0), LINES)
    )
    offsets = jnp.dot(jnp.where(above, 1.0, 0.0).astype(BF16), totals.astype(BF16), preferred_element_type=F32)
    rank = within + offsets

    slot = iota((SLOTS, 128), 0).astype(F32)
    lane_sum = jnp.full((LINES, 128), -1.0, F32)
    line_sum = jnp.full((LINES, 128), -1.0, F32)
    counts = []
    for b in range(4):
        mine = rank[b * LINES : (b + 1) * LINES]
        position = jnp.where(member[b] > 0, mine, -1.0)
        for r in range(LINES):
            pick[b * SLOTS : (b + 1) * SLOTS, r * 128 : (r + 1) * 128] = jnp.where(
                slot == position[r : r + 1], 1.0, 0.0
            ).astype(BF16)
        counts.append(jnp.sum(totals[b * LINES : (b + 1) * LINES], axis=0, keepdims=True))
        stage = jnp.floor(mine * (1.0 / PIECE))
        shift = (column[b] * PIECE).astype(F32)
        lane_sum = jnp.where(member[b] > 0, mine - stage * PIECE + shift, lane_sum)
        line_sum = jnp.where(member[b] > 0, stage + b * STAGES, line_sum)
    lane_of[...] = lane_sum
    line_of[...] = line_sum

    load.wait()

    def gather(n, carry):
        cols = pl.ds(pl.multiple_of(n * COLS, COLS), COLS)
        gathered[:, cols] = jnp.dot(pick[...], rows[:, cols], preferred_element_type=F32)
        return carry

    lax.fori_loop(0, WIDTH // COLS, gather, 0)

    for b in range(4):
        span = slice(b * SLOTS, (b + 1) * SLOTS)
        values = gathered[span, :]
        inverse = lax.rsqrt(jnp.sum(values * values, axis=1, keepdims=True) + EPSILON)
        unit = (values * inverse).astype(BF16)
        blocks[span, :] = unit
        empty = (slot >= counts[b]) & (iota((SLOTS, 128), 1) == 0)
        head = values[:, 0:128] * inverse
        blocks[span, 0:128] = jnp.where(empty, PADDED, head).astype(BF16)

    @pl.when(role == 0)
    def _():
        pl.semaphore_wait(barrier, PLANES + 3)

    @pl.when(role != 0)
    def _():
        pl.semaphore_wait(barrier, PLANES + 4)

    def member_rows(t, half, source):
        return members.at[pl.ds(pl.multiple_of(t * STAGE_ROWS + half * HALF + source * PIECE, PIECE), PIECE)]

    def relay_rows(t, dx):
        return relay.at[pl.ds(pl.multiple_of((t * SIDE + dx) * PIECE, PIECE), PIECE)]

    def block_rows(t, b):
        return blocks.at[pl.ds(pl.multiple_of(b * SLOTS + t * PIECE, PIECE), PIECE)]

    def send(t, b):
        if b < 2:
            dst = member_rows(t, core, SIDE * b + column[b])
            sem = arrive.at[t, SIDE * b + column[b]]
        else:
            dst = relay_rows(t, column[b])
            sem = relay_arrive.at[t, column[b]]
        return pltpu.make_async_remote_copy(
            src_ref=block_rows(t, b), dst_ref=dst, send_sem=sent.at[t, b], recv_sem=sem,
            device_id=(target[b], z), device_id_type=MESH,
        )

    def keep(t):
        return pltpu.make_async_copy(block_rows(t, 0), member_rows(t, core, 0), arrive.at[t, 0])

    def start_sends(t):
        send(t, 3).start()
        send(t, 2).start()
        send(t, 1).start()

        @pl.when(role != 0)
        def _():
            send(t, 0).start()

        @pl.when(role == 0)
        def _():
            keep(t).start()

    def end_sends(t):
        send(t, 3).wait_send()
        send(t, 2).wait_send()
        send(t, 1).wait_send()

        @pl.when(role != 0)
        def _():
            send(t, 0).wait_send()

    row_of_relay = 2 + lax.div(3 - role, 2)
    plane_of_relay = lax.rem(z + 1 + (3 - role) * 3, PLANES)

    def forward(t, dx):
        source = SIDE * row_of_relay + dx
        return pltpu.make_async_remote_copy(
            src_ref=relay_rows(t, dx), dst_ref=member_rows(t, core, source),
            send_sem=forwarded.at[t, dx], recv_sem=arrive.at[t, source],
            device_id=(docs, plane_of_relay), device_id_type=MESH,
        )

    def arrival(t, source):
        return pltpu.make_async_copy(member_rows(t, core, source), member_rows(t, core, source), arrive.at[t, source])

    def relay_arrival(t, dx):
        return pltpu.make_async_copy(relay_rows(t, dx), relay_rows(t, dx), relay_arrive.at[t, dx])

    def swap(t, half):
        span = pl.ds(pl.multiple_of(t * STAGE_ROWS + half * HALF, HALF), HALF)
        return pltpu.make_async_remote_copy(
            src_ref=members.at[span], dst_ref=members.at[span], send_sem=swap_sent.at[t], recv_sem=swap_arrive.at[t],
            device_id=(sibling, z), device_id_type=MESH,
        )

    start_sends(0)
    start_sends(1)

    @pl.when(role == 0)
    def _():
        col_max[...] = jnp.full(col_max.shape, LOWEST, F32)
        answer[...] = jnp.full(answer.shape, LOWEST, F32)

    def compute(t):
        base = pl.multiple_of(t * STAGE_ROWS + core * HALF, HALF)
        first = members[pl.ds(base, HALF), 0:128].astype(F32)[:, 0:1]
        row_bias[...] = jnp.broadcast_to(jnp.where(first > 1.5, FAR, 0.0), (HALF, 128))
        row_max[...] = jnp.full(row_max.shape, LOWEST, F32)

        def scores(start):
            return lax.dot_general(
                members[pl.ds(base, HALF), :], members[pl.ds(start, COLS), :], NT, preferred_element_type=F32
            )

        def along_rows(score, bias):
            biased = score + bias
            best = row_max[...]
            for c in range(0, COLS, 128):
                best = jnp.maximum(best, biased[:, c : c + 128])
            row_max[...] = best

        def old(n, carry):
            start = pl.multiple_of(n * COLS, COLS)
            score = scores(start)
            along_rows(score, col_bias[0:1, pl.ds(start, COLS)])
            for c in range(0, COLS, 128):
                biased = (score[:, c : c + 128] + row_bias[...]).reshape(HALF // 8, 8, 128)
                cols = pl.ds(pl.multiple_of(start + c, 128), 128)
                col_max[:, cols] = jnp.maximum(col_max[:, cols], jnp.max(biased, axis=0))
            return carry

        def mark(start):
            chosen = jnp.where((iota((16, 128), 0) < 8) & (iota((16, 128), 1) == 0), 1.0, 0.0).astype(BF16)
            heads = lax.dot_general(chosen, members[pl.ds(start, COLS), 0:128], NT, preferred_element_type=F32)
            bias = jnp.where(heads[0:8] > 1.5, FAR, 0.0)
            col_bias[:, pl.ds(start, COLS)] = bias
            return bias[0:1]

        def own(n, carry):
            start = pl.multiple_of(base + n * COLS, COLS)
            same = iota((HALF, COLS), 0) == iota((HALF, COLS), 1) + n * COLS
            along_rows(jnp.where(same, LOWEST, scores(start)), mark(start))
            return carry

        def other(n, carry):
            start = pl.multiple_of(t * STAGE_ROWS + (1 - core) * HALF + n * COLS, COLS)
            along_rows(scores(start), mark(start))
            return carry

        lax.fori_loop(0, t * (STAGE_ROWS // COLS), old, 0)
        lax.fori_loop(0, HALF // COLS, own, 0)
        swap(t, 1 - core).wait_recv()
        lax.fori_loop(0, HALF // COLS, other, 0)
        for dy in range(SIDE):
            turned = row_max[dy * 128 : (dy + 1) * 128, :].T
            row_best[pl.ds(t * SIDE + dy, 1), :] = jnp.max(turned, axis=0, keepdims=True)

    def stage_body(t, carry):
        @pl.when((role == 3) | (role == 1))
        def _():
            for dx in range(SIDE):
                relay_arrival(t, dx).wait()
                forward(t, dx).start()

        @pl.when(role == 0)
        def _():
            for source in range(SOURCES):
                arrival(t, source).wait()
            swap(t, core).start()
            compute(t)

        end_sends(t)

        @pl.when(t + 2 < STAGES)
        def _():
            start_sends(t + 2)

        return carry

    lax.fori_loop(0, STAGES, stage_body, 0)

    source_plane = [z, z, plane(z - 1), plane(z + 1)]

    def give(half, dy, dx, device):
        return pltpu.make_async_remote_copy(
            src_ref=answer.at[half, dy], dst_ref=returned.at[dy, core],
            send_sem=back_sent.at[half, dy, dx], recv_sem=back_arrive.at[dy, core],
            device_id=(device, source_plane[dy]), device_id_type=MESH,
        )

    def gives():
        copies = [give(1 - core, 0, 0, sibling)]
        for dy in range(SIDE):
            for dx in range(SIDE):
                if dx or dy:
                    for half in range(2):
                        copies.append(give(half, dy, dx, place(x + dx, y + dy, half)))
        return copies

    @pl.when(role == 0)
    def _():
        for t in range(STAGES):
            for half in range(2):
                for dy in range(SIDE):
                    start = t * STAGE_ROWS + half * HALF + dy * 128
                    best = jnp.max(col_max[:, start : start + 128], axis=0, keepdims=True)
                    mine = row_best[t * SIDE + dy : t * SIDE + dy + 1, :]
                    answer[half, dy, t : t + 1] = jnp.where(core == half, jnp.maximum(best, mine), best)
        for copy in gives():
            copy.start()
        pltpu.make_async_copy(answer.at[core, 0], returned.at[0, core], back_arrive.at[0, core]).start()

    for b in range(4):
        for half in range(2):
            pltpu.make_async_copy(returned.at[b, half], returned.at[b, half], back_arrive.at[b, half]).wait()

    found = jnp.concatenate(
        [jnp.maximum(returned[b, 0], returned[b, 1])[0:STAGES] for b in range(4)], axis=0
    )
    high = found.astype(BF16)
    rest = found - high.astype(F32)
    middle = rest.astype(BF16)
    low = (rest - middle.astype(F32)).astype(BF16)
    parts = jnp.concatenate([high, middle, low], axis=0)
    lane = iota((128, 128), 0).astype(F32)
    line = iota((16, 128), 0).astype(F32)
    for r in range(LINES):
        chosen = jnp.where(lane == lane_of[r : r + 1, :], 1.0, 0.0).astype(BF16)
        taken = jnp.dot(parts, chosen, preferred_element_type=F32)
        taken = taken[0:16] + taken[16:32] + taken[32:48]
        partial[z, r : r + 1] = jnp.sum(
            jnp.where(line == line_of[r : r + 1, :], taken, 0.0), axis=0, keepdims=True
        )

    def share(step):
        return pltpu.make_async_remote_copy(
            src_ref=partial.at[z], dst_ref=partial.at[z],
            send_sem=part_sent.at[step], recv_sem=part_arrive.at[step],
            device_id=(docs, plane(z + step)), device_id_type=MESH,
        )

    for step in range(1, PLANES):
        share(step).start()
    for step in range(1, PLANES):
        slot_of = partial.at[plane(z - step)]
        pltpu.make_async_copy(slot_of, slot_of, part_arrive.at[step]).wait()
    total = partial[0]
    for step in range(1, PLANES):
        total = total + partial[step]
    out_ref[...] = total

    for step in range(1, PLANES):
        share(step).wait_send()

    @pl.when((role == 3) | (role == 1))
    def _():
        for t in range(STAGES):
            for dx in range(SIDE):
                forward(t, dx).wait_send()

    @pl.when(role == 0)
    def _():
        for t in range(STAGES):
            swap(t, core).wait_send()
        for copy in gives():
            copy.wait_send()


def local(embeds, cluster_of):
    dma = pltpu.SemaphoreType.DMA
    out = pl.pallas_call(
        kernel,
        out_shape=jax.ShapeDtypeStruct((LINES, 128), F32),
        in_specs=[pl.BlockSpec(memory_space=pltpu.VMEM), pl.BlockSpec(memory_space=pl.ANY)],
        out_specs=pl.BlockSpec(memory_space=pltpu.VMEM),
        scratch_shapes=[
            pltpu.VMEM((DOCS, WIDTH), BF16),
            pltpu.VMEM((4 * SLOTS, DOCS), BF16),
            pltpu.VMEM((4 * SLOTS, WIDTH), F32),
            pltpu.VMEM((4 * SLOTS, WIDTH), BF16),
            pltpu.VMEM((4 * SLOTS, WIDTH), BF16),
            pltpu.VMEM((MEMBERS, WIDTH), BF16),
            pltpu.VMEM((HALF, 128), F32),
            pltpu.VMEM((8, MEMBERS), F32),
            pltpu.VMEM((HALF, 128), F32),
            pltpu.VMEM((8, MEMBERS), F32),
            pltpu.VMEM((STAGES * SIDE, 128), F32),
            pltpu.VMEM((2, SIDE, 8, 128), F32),
            pltpu.VMEM((4, 2, 8, 128), F32),
            pltpu.VMEM((PLANES, LINES, 128), F32),
            pltpu.VMEM((LINES, 128), F32),
            pltpu.VMEM((LINES, 128), F32),
            dma,
            dma((STAGES, 4)),
            dma((STAGES, SIDE)),
            dma((STAGES, SIDE)),
            dma((STAGES, SOURCES)),
            dma((STAGES,)),
            dma((STAGES,)),
            dma((2, SIDE, SIDE)),
            dma((4, 2)),
            dma((PLANES,)),
            dma((PLANES,)),
        ],
        compiler_params=pltpu.CompilerParams(
            collective_id=0, has_side_effects=True, vmem_limit_bytes=48 * 2**20
        ),
        cost_estimate=pl.CostEstimate(flops=13 * 10**9, bytes_accessed=4 * 2**20, transcendentals=512),
    )(cluster_of.reshape(LINES, 128), embeds)
    return out.reshape(DOCS)


def solution(mesh):
    return jax.shard_map(
        local,
        mesh=mesh,
        in_specs=(P("docs", None), P("docs")),
        out_specs=P("docs"),
        check_vma=False,
    )
```

time: 241 us -> 75.1 us (0.31)
  waiting for transfers between devices: 99.6 us -> 0 us
  Pallas kernels: 0 us -> 71.5 us
  blocking collectives: 48.8 us -> 0 us
  local copies, waits for them, and re-layouts: 36.5 us -> 3.48 us
  other arithmetic: 30.6 us -> 0 us
  starting transfers between devices: 16 us -> 0 us
  matrix products: 9.1 us -> 0 us
    all_to_all x2 -> x0, waiting for transfers between devices: 99.6 us -> none  [the longest x1 99.6 us: local(): lax.all_to_all(outgoing, 'docs', split_axis=0, concat_axis=0, tiled=True)]
    pallas_call x0 -> x1, Pallas kernels: none -> 71.5 us  [local(): pl.pallas_call(kernel, out_shape=jax.ShapeDtypeStruct((LINES, 128), F32),...]
    pmax x1 -> x0, blocking collectives: 25.5 us -> none  [local(): nearest_slot = lax.pmax(nearest_slot, 'grp')]
    all_to_all x1 -> x0, blocking collectives: 23.3 us -> none  [local(): lax.all_to_all(nearest_slot.reshape(doc_groups, slot_count), 'docs', spli...]
    gather x1 -> x0, local copies, waits for them, and re-layouts: 20.5 us -> none  [local(): return returned.reshape(-1)[position]]
    all_to_all x2 -> x0, starting transfers between devices: 16 us -> none  [the longest x1 8.59 us: local(): lax.all_to_all(present, 'docs', split_axis=0, concat_axis=0, tiled=True)]
    scatter x1 -> x0, other arithmetic: 15.8 us -> none  [local(): jnp.zeros((capacity, feature_count), jnp.bfloat16).at[position]]
    scatter x1 -> x0, local copies, waits for them, and re-layouts: 14.6 us -> none  [local(): jnp.zeros((capacity,), jnp.bfloat16).at[position]]
  transfers between devices with their start and end apart: 2 -> 0, of which waited for: 1 -> 0; matrix products, arithmetic and copies ran while one was open for 8% -> 0% of each run, Pallas kernels for 0% -> 0%
where the time goes in v1:
time: 75.1 us; the launch traced here: 75 us
  Pallas kernels  71.5 us (95%)
  local copies, waits for them, and re-layouts  3.48 us (5%)
    pallas_call x1, Pallas kernels, local(): pl.pallas_call(kernel, out_shape=jax.ShapeDtypeStruct((LINES, 128), F32),...  71.5 us
    unnamed x5, local copies, waits for them, and re-layouts  3.48 us

profile of v1, /device:TPU:1, one launch (start us, length us, event | category | flops | bytes accessed | tf_op | source)
XLA Modules:
  0.0 75.0 jit_solution(4114633601095634443)
XLA Ops:
  0.0 0.0 copy-start
  0.0 2.2 %copy-done = bf16[2048,1024]{1,0:T(8,128)(2,1)S(1)} copy-done((bf16[2048,1024]{1,0:T(8,128)(2,1)S(1)}, bf16[2048,1024]{1,0:T(8,128)(2,1)}, u32[]{:S(2)}) %copy-start) | copy-done | bytes 4194328
  2.2 0.0 copy-start.1
  2.2 0.7 copy-done.1
  2.9 71.5 %shard_map.28 = f32[16,128]{1,0:T(8,128)S(1)} custom-call(s32[16,128]{1,0:T(8,128)S(1)} %bitcast.3, bf16[2048,1024]{1,0:T(8,128)(2,1)S(1)} %copy-done), custom_call_target="tpu_custom_call" | custom-call | flops 12999999488 | bytes 4194304 | tf_op jit(solution)/shard_map/pallas_call | solution.py:393
  74.4 0.6 copy.4
Async XLA Ops:
  0.0 2.2 %copy-start = (bf16[2048,1024]{1,0:T(8,128)(2,1)S(1)}, bf16[2048,1024]{1,0:T(8,128)(2,1)}, u32[]{:S(2)}) copy-start(bf16[2048,1024]{1,0:T(8,128)(2,1)} %embeds_ref.1) | copy-start | bytes 12582916
  2.2 0.7 copy-start.1

commit v2 on v1

v2 whole, which is shorter than its diff:
```python
import jax
import jax.numpy as jnp
from jax import lax
from jax.experimental import pallas as pl
from jax.experimental.pallas import tpu as pltpu
from jax.sharding import PartitionSpec as P


EPSILON = 1e-06
LOWEST = -3e38
FAR = -1e30
PADDED = 2.0

SIDE = 4
PLANES = 8
DOCS = 2048
WIDTH = 1024
SLOTS = 128
STAGES = 4
PIECE = SLOTS // STAGES
GROUP = SIDE * PIECE
STAGE_ROWS = 4 * GROUP
MEMBERS = STAGES * STAGE_ROWS
COLS = 256
LINES = DOCS // 128
OTHER, OWN, NEXT, PREVIOUS = range(4)

MESH = pl.DeviceIdType.MESH
F32 = jnp.float32
BF16 = jnp.bfloat16
NT = (((1,), (1,)), ((), ()))


def iota(shape, axis):
    return lax.broadcasted_iota(jnp.int32, shape, axis)


def kernel(
    cluster_ref, embeds_ref, out_ref,
    rows, pick, gathered, blocks, members, row_bias, col_bias, row_max, col_max, row_best, answer,
    returned, partial, lane_of, line_of,
    load_sem, shipped, arrive, passed, near_arrive, swap_sent, swap_arrive, back_sent, back_arrive,
    part_sent, part_arrive, hello,
):
    docs = lax.axis_index("docs")
    z = lax.axis_index("grp")
    core = lax.rem(docs, 2)
    x = lax.rem(lax.div(docs, 2), SIDE)
    y = lax.div(docs, 2 * SIDE)

    def place(px, py, pcore):
        return (lax.rem(py + SIDE, SIDE) * SIDE + lax.rem(px, SIDE)) * 2 + lax.rem(pcore, 2)

    def plane(pz):
        return lax.rem(pz + PLANES, PLANES)

    def turn(py):
        return lax.div(lax.rem(py + 3, SIDE), 2)

    sibling = place(x, y, core + 1)
    ahead = place(x, y + 1, core + turn(y + 1))
    behind = place(x, y - 1, core)
    from_ahead = place(x, y + 1, core)
    from_behind = place(x, y - 1, core + turn(y))

    load = pltpu.make_async_copy(embeds_ref, rows, load_sem)
    load.start()

    barrier = pltpu.get_barrier_semaphore()

    def greet(device):
        pl.semaphore_signal(barrier, inc=1, device_id=device, device_id_type=MESH)

    for step in range(1, SIDE):
        greet((place(x + step, y, core), z))
    greet((from_ahead, z))
    greet((from_behind, z))
    greet((sibling, z))
    greet((docs, plane(z + 1)))
    greet((docs, plane(z - 1)))

    clusters = cluster_ref[...]
    member = [jnp.where(clusters == SIDE * z + b, 1.0, 0.0).astype(F32) for b in range(4)]
    stacked = jnp.concatenate(member, axis=0).astype(BF16)
    before = jnp.where(iota((128, 128), 0) < iota((128, 128), 1), 1.0, 0.0).astype(BF16)
    within = jnp.dot(stacked, before, preferred_element_type=F32)
    totals = jnp.dot(stacked, jnp.ones((128, 128), BF16), preferred_element_type=F32)
    lines = 4 * LINES
    above = (iota((lines, lines), 1) < iota((lines, lines), 0)) & (
        lax.div(iota((lines, lines), 1), LINES) == lax.div(iota((lines, lines), 0), LINES)
    )
    offsets = jnp.dot(jnp.where(above, 1.0, 0.0).astype(BF16), totals.astype(BF16), preferred_element_type=F32)
    rank = within + offsets

    slot = iota((SLOTS, 128), 0).astype(F32)
    lane_sum = jnp.full((LINES, 128), -1.0, F32)
    line_sum = jnp.full((LINES, 128), -1.0, F32)
    counts = []
    for b in range(4):
        mine = rank[b * LINES : (b + 1) * LINES]
        position = jnp.where(member[b] > 0, mine, -1.0)
        for r in range(LINES):
            pick[b * SLOTS : (b + 1) * SLOTS, r * 128 : (r + 1) * 128] = jnp.where(
                slot == position[r : r + 1], 1.0, 0.0
            ).astype(BF16)
        counts.append(jnp.sum(totals[b * LINES : (b + 1) * LINES], axis=0, keepdims=True))
        stage = jnp.floor(mine * (1.0 / PIECE))
        lane_sum = jnp.where(member[b] > 0, mine - stage * PIECE + (x * PIECE).astype(F32), lane_sum)
        line_sum = jnp.where(member[b] > 0, stage + b * STAGES, line_sum)
    lane_of[...] = lane_sum
    line_of[...] = line_sum

    load.wait()

    def gather(n, carry):
        cols = pl.ds(pl.multiple_of(n * COLS, COLS), COLS)
        gathered[:, cols] = jnp.dot(pick[...], rows[:, cols], preferred_element_type=F32)
        return carry

    lax.fori_loop(0, WIDTH // COLS, gather, 0)

    for b in range(4):
        span = slice(b * SLOTS, (b + 1) * SLOTS)
        values = gathered[span, :]
        inverse = lax.rsqrt(jnp.sum(values * values, axis=1, keepdims=True) + EPSILON)
        unit = (values * inverse).astype(BF16)
        blocks[span, :] = unit
        empty = (slot >= counts[b]) & (iota((SLOTS, 128), 1) == 0)
        head = values[:, 0:128] * inverse
        blocks[span, 0:128] = jnp.where(empty, PADDED, head).astype(BF16)

    pl.semaphore_wait(barrier, SIDE + 4)

    def group_rows(t, group):
        return pl.ds(pl.multiple_of(t * STAGE_ROWS + group * GROUP, GROUP), GROUP)

    def piece(t, group, source):
        return members.at[pl.ds(pl.multiple_of(t * STAGE_ROWS + group * GROUP + source * PIECE, PIECE), PIECE)]

    def block(t, b):
        return blocks.at[pl.ds(pl.multiple_of(b * SLOTS + t * PIECE, PIECE), PIECE)]

    def arrival(ref, sem):
        return pltpu.make_async_copy(ref, ref, sem)

    def ship(t, step):
        column = lax.rem(x + step, SIDE)
        return pltpu.make_async_remote_copy(
            src_ref=block(t, column), dst_ref=piece(t, OWN, x),
            send_sem=shipped.at[t, step], recv_sem=arrive.at[t, x],
            device_id=(place(column, y, core), z), device_id_type=MESH,
        )

    def pass_on(t, source, src, group):
        return pltpu.make_async_remote_copy(
            src_ref=src, dst_ref=piece(t, group, source),
            send_sem=passed.at[t, source, group - NEXT], recv_sem=near_arrive.at[t, source, group - NEXT],
            device_id=(behind if group == NEXT else ahead, z), device_id_type=MESH,
        )

    def pass_both(t, source, src):
        pass_on(t, source, src, NEXT).start()
        pass_on(t, source, src, PREVIOUS).start()

    def swap(t):
        return pltpu.make_async_remote_copy(
            src_ref=members.at[group_rows(t, OWN)], dst_ref=members.at[group_rows(t, OTHER)],
            send_sem=swap_sent.at[t], recv_sem=swap_arrive.at[t],
            device_id=(sibling, z), device_id_type=MESH,
        )

    def start_ships(t):
        pass_both(t, x, block(t, x))
        for step in (2, 3, 1):
            ship(t, step).start()
        pltpu.make_async_copy(block(t, x), piece(t, OWN, x), arrive.at[t, x]).start()

    def end_ships(t):
        for step in (2, 3, 1):
            ship(t, step).wait_send()

    def relay(t):
        for step in (3, 1, 2):
            source = lax.rem(x + step, SIDE)
            arrival(piece(t, OWN, source), arrive.at[t, source]).wait()
            pass_both(t, source, piece(t, OWN, source))
        arrival(piece(t, OWN, x), arrive.at[t, x]).wait()
        swap(t).start()

    def compute(t):
        base = pl.multiple_of(t * STAGE_ROWS, STAGE_ROWS)
        first = members[pl.ds(base, STAGE_ROWS), 0:128].astype(F32)[:, 0:1]
        row_bias[...] = jnp.broadcast_to(jnp.where(first > 1.5, FAR, 0.0), (STAGE_ROWS, 128))
        row_max[...] = jnp.full(row_max.shape, LOWEST, F32)

        def scores(start):
            return lax.dot_general(
                members[pl.ds(base, STAGE_ROWS), :], members[pl.ds(start, COLS), :], NT, preferred_element_type=F32
            )

        def along_rows(score, bias):
            biased = score + bias
            best = row_max[...]
            for c in range(0, COLS, 128):
                best = jnp.maximum(best, biased[:, c : c + 128])
            row_max[...] = best

        def old(n, carry):
            start = pl.multiple_of(n * COLS, COLS)
            score = scores(start)
            along_rows(score, col_bias[0:1, pl.ds(start, COLS)])
            for c in range(0, COLS, 128):
                biased = (score[:, c : c + 128] + row_bias[...]).reshape(STAGE_ROWS // 8, 8, 128)
                cols = pl.ds(pl.multiple_of(start + c, 128), 128)
                col_max[:, cols] = jnp.maximum(col_max[:, cols], jnp.max(biased, axis=0))
            return carry

        def mark(start):
            chosen = jnp.where((iota((16, 128), 0) < 8) & (iota((16, 128), 1) == 0), 1.0, 0.0).astype(BF16)
            heads = lax.dot_general(chosen, members[pl.ds(start, COLS), 0:128], NT, preferred_element_type=F32)
            bias = jnp.where(heads[0:8] > 1.5, FAR, 0.0)
            col_bias[:, pl.ds(start, COLS)] = bias
            return bias[0:1]

        def new(n, carry):
            start = pl.multiple_of(base + n * COLS, COLS)
            same = iota((STAGE_ROWS, COLS), 0) == iota((STAGE_ROWS, COLS), 1) + n * COLS
            along_rows(jnp.where(same, LOWEST, scores(start)), mark(start))
            return carry

        lax.fori_loop(0, t * (STAGE_ROWS // COLS), old, 0)
        lax.fori_loop(0, STAGE_ROWS // COLS, new, 0)
        for group in range(4):
            turned = row_max[group * GROUP : (group + 1) * GROUP, :].T
            row_best[pl.ds(t * 4 + group, 1), :] = jnp.max(turned, axis=0, keepdims=True)

    start_ships(0)
    start_ships(1)
    col_max[...] = jnp.full(col_max.shape, LOWEST, F32)
    answer[...] = jnp.full(answer.shape, LOWEST, F32)

    for turn_of in range(3):
        for step in (1, -1):
            pl.semaphore_signal(hello.at[turn_of], inc=1, device_id=(docs, plane(z + step)), device_id_type=MESH)
        pl.semaphore_wait(hello.at[turn_of], 2)

    relay(0)

    def stage_body(t, carry):
        end_ships(t)

        @pl.when(t + 2 < STAGES)
        def _():
            start_ships(t + 2)

        @pl.when(t + 1 < STAGES)
        def _():
            relay(t + 1)

        for source in range(SIDE):
            for group in (NEXT, PREVIOUS):
                arrival(piece(t, group, source), near_arrive.at[t, source, group - NEXT]).wait()
        swap(t).wait_recv()
        compute(t)
        return carry

    lax.fori_loop(0, STAGES, stage_body, 0)

    for t in range(STAGES):
        for group in range(4):
            start = t * STAGE_ROWS + group * GROUP
            best = jnp.max(col_max[:, start : start + GROUP], axis=0, keepdims=True)
            mine = row_best[t * 4 + group : t * 4 + group + 1, :]
            answer[group, t : t + 1] = jnp.maximum(best, mine)

    def give(group, step):
        column = x + step
        device = [
            place(column, y, core + 1), place(column, y, core),
            place(column, y + 1, core), place(column, y - 1, core + turn(y)),
        ][group]
        return pltpu.make_async_remote_copy(
            src_ref=answer.at[group], dst_ref=returned.at[x, group],
            send_sem=back_sent.at[group, step], recv_sem=back_arrive.at[x, group],
            device_id=(device, z), device_id_type=MESH,
        )

    gives = [give(group, step) for step in (2, 1, 3, 0) for group in range(4) if step or group != OWN]
    for copy in gives:
        copy.start()
    pltpu.make_async_copy(answer.at[OWN], returned.at[x, OWN], back_arrive.at[x, OWN]).start()
    for b in range(4):
        for group in range(4):
            arrival(returned.at[b, group], back_arrive.at[b, group]).wait()

    found = jnp.concatenate(
        [
            jnp.maximum(
                jnp.maximum(returned[b, 0], returned[b, 1]), jnp.maximum(returned[b, 2], returned[b, 3])
            )[0:STAGES]
            for b in range(4)
        ],
        axis=0,
    )
    high = found.astype(BF16)
    rest = found - high.astype(F32)
    middle = rest.astype(BF16)
    low = (rest - middle.astype(F32)).astype(BF16)
    parts = jnp.concatenate([high, middle, low], axis=0)
    lane = iota((128, 128), 0).astype(F32)
    line = iota((16, 128), 0).astype(F32)
    for r in range(LINES):
        chosen = jnp.where(lane == lane_of[r : r + 1, :], 1.0, 0.0).astype(BF16)
        taken = jnp.dot(parts, chosen, preferred_element_type=F32)
        taken = taken[0:16] + taken[16:32] + taken[32:48]
        partial[z, r : r + 1] = jnp.sum(
            jnp.where(line == line_of[r : r + 1, :], taken, 0.0), axis=0, keepdims=True
        )

    def share(step):
        return pltpu.make_async_remote_copy(
            src_ref=partial.at[z], dst_ref=partial.at[z],
            send_sem=part_sent.at[step], recv_sem=part_arrive.at[step],
            device_id=(docs, plane(z + step)), device_id_type=MESH,
        )

    for step in range(1, PLANES):
        share(step).start()
    for step in range(1, PLANES):
        slot_of = partial.at[plane(z - step)]
        pltpu.make_async_copy(slot_of, slot_of, part_arrive.at[step]).wait()
    total = partial[0]
    for step in range(1, PLANES):
        total = total + partial[step]
    out_ref[...] = total

    for step in range(1, PLANES):
        share(step).wait_send()

    for copy in gives:
        copy.wait_send()

    def end_stage(t, carry):
        swap(t).wait_send()
        for source in range(SIDE):
            for group in (NEXT, PREVIOUS):
                pass_on(t, source, piece(t, OWN, source), group).wait_send()
        return carry

    lax.fori_loop(0, STAGES, end_stage, 0)


def local(embeds, cluster_of):
    dma = pltpu.SemaphoreType.DMA
    out = pl.pallas_call(
        kernel,
        out_shape=jax.ShapeDtypeStruct((LINES, 128), F32),
        in_specs=[pl.BlockSpec(memory_space=pltpu.VMEM), pl.BlockSpec(memory_space=pl.ANY)],
        out_specs=pl.BlockSpec(memory_space=pltpu.VMEM),
        scratch_shapes=[
            pltpu.VMEM((DOCS, WIDTH), BF16),
            pltpu.VMEM((4 * SLOTS, DOCS), BF16),
            pltpu.VMEM((4 * SLOTS, WIDTH), F32),
            pltpu.VMEM((4 * SLOTS, WIDTH), BF16),
            pltpu.VMEM((MEMBERS, WIDTH), BF16),
            pltpu.VMEM((STAGE_ROWS, 128), F32),
            pltpu.VMEM((8, MEMBERS), F32),
            pltpu.VMEM((STAGE_ROWS, 128), F32),
            pltpu.VMEM((8, MEMBERS), F32),
            pltpu.VMEM((STAGES * 4, 128), F32),
            pltpu.VMEM((4, 8, 128), F32),
            pltpu.VMEM((4, 4, 8, 128), F32),
            pltpu.VMEM((PLANES, LINES, 128), F32),
            pltpu.VMEM((LINES, 128), F32),
            pltpu.VMEM((LINES, 128), F32),
            dma,
            dma((STAGES, SIDE)),
            dma((STAGES, SIDE)),
            dma((STAGES, SIDE, 2)),
            dma((STAGES, SIDE, 2)),
            dma((STAGES,)),
            dma((STAGES,)),
            dma((4, SIDE)),
            dma((4, 4)),
            dma((PLANES,)),
            dma((PLANES,)),
            pltpu.SemaphoreType.REGULAR((3,)),
        ],
        compiler_params=pltpu.CompilerParams(
            collective_id=0, has_side_effects=True, vmem_limit_bytes=48 * 2**20
        ),
        cost_estimate=pl.CostEstimate(flops=8 * 10**9, bytes_accessed=4 * 2**20, transcendentals=512),
    )(cluster_of.reshape(LINES, 128), embeds)
    return out.reshape(DOCS)


def solution(mesh):
    return jax.shard_map(
        local,
        mesh=mesh,
        in_specs=(P("docs", None), P("docs")),
        out_specs=P("docs"),
        check_vma=False,
    )
```

time: 75.1 us -> 56.9 us (0.76)
  Pallas kernels: 71.5 us -> 53.3 us
    pallas_call x1, Pallas kernels: 71.5 us -> 53.3 us  [local(): pl.pallas_call(kernel, out_shape=jax.ShapeDtypeStruct((LINES, 128), F32),...]
where the time goes in v2:
time: 56.9 us; the launch traced here: 56.8 us
  Pallas kernels  53.3 us (94%)
  local copies, waits for them, and re-layouts  3.48 us (6%)
    pallas_call x1, Pallas kernels, local(): pl.pallas_call(kernel, out_shape=jax.ShapeDtypeStruct((LINES, 128), F32),...  53.3 us
    unnamed x5, local copies, waits for them, and re-layouts  3.48 us

profile of v2, /device:TPU:1, one launch (start us, length us, event | category | flops | bytes accessed | tf_op | source)
XLA Modules:
  0.0 56.8 jit_solution(158024530627068677)
XLA Ops:
  0.0 0.0 copy-start
  0.0 2.2 %copy-done = bf16[2048,1024]{1,0:T(8,128)(2,1)S(1)} copy-done((bf16[2048,1024]{1,0:T(8,128)(2,1)S(1)}, bf16[2048,1024]{1,0:T(8,128)(2,1)}, u32[]{:S(2)}) %copy-start) | copy-done | bytes 4194328
  2.2 0.0 copy-start.1
  2.2 0.7 %copy-done.1 = s32[2048]{0:T(1024)S(1)} copy-done((s32[2048]{0:T(1024)S(1)}, s32[2048]{0:T(1024)}, u32[]{:S(2)}) %copy-start.1) | copy-done | bytes 8216
  2.9 53.3 %shard_map.28 = f32[16,128]{1,0:T(8,128)S(1)} custom-call(s32[16,128]{1,0:T(8,128)S(1)} %bitcast.3, bf16[2048,1024]{1,0:T(8,128)(2,1)S(1)} %copy-done), custom_call_target="tpu_custom_call" | custom-call | flops 8000000000 | bytes 4194304 | tf_op jit(solution)/shard_map/pallas_call | solution.py:355
  56.2 0.6 %copy.4 = f32[2048]{0:T(1024)} copy(f32[2048]{0:T(1024)S(1)} %bitcast.2) | data formatting | bytes 16384
Async XLA Ops:
  0.0 2.2 %copy-start = (bf16[2048,1024]{1,0:T(8,128)(2,1)S(1)}, bf16[2048,1024]{1,0:T(8,128)(2,1)}, u32[]{:S(2)}) copy-start(bf16[2048,1024]{1,0:T(8,128)(2,1)} %embeds_ref.1) | copy-start | bytes 12582916
  2.2 0.7 %copy-start.1 = (s32[2048]{0:T(1024)S(1)}, s32[2048]{0:T(1024)}, u32[]{:S(2)}) copy-start(s32[2048]{0:T(1024)} %param.3) | copy-start | bytes 24580

commit v3 on v2

v3 whole, which is shorter than its diff:
```python
import jax
import jax.numpy as jnp
from jax import lax
from jax.experimental import pallas as pl
from jax.experimental.pallas import tpu as pltpu
from jax.sharding import PartitionSpec as P


EPSILON = 1e-06
LOWEST = -3e38
FAR = -1e30
PADDED = 2.0

SIDE = 4
PLANES = 8
CLUSTERS = SIDE * PLANES
DOCS = 2048
WIDTH = 1024
SLOTS = 128
STAGES = 4
PIECE = SLOTS // STAGES
GROUP = SIDE * PIECE
REGION = STAGES * GROUP
MEMBERS = 4 * REGION
EARLY = PIECE
LINES = DOCS // 128
OWN, OTHER, PREVIOUS, NEXT = range(4)

MESH = pl.DeviceIdType.MESH
F32 = jnp.float32
BF16 = jnp.bfloat16
NT = (((1,), (1,)), ((), ()))


def iota(shape, axis):
    return lax.broadcasted_iota(jnp.int32, shape, axis)


def kernel(
    cluster_ref, embeds_ref, out_ref,
    rows, pick, gathered, blocks, members, col_bias, row_max, col_max, answer,
    near, final, returned, rank_of,
    load_sem, shipped, arrive, passed, near_arrive, swap_sent, swap_arrive, near_sent, back_near, back_sent,
    back_arrive, hello,
):
    docs = lax.axis_index("docs")
    z = lax.axis_index("grp")
    core = lax.rem(docs, 2)
    x = lax.rem(lax.div(docs, 2), SIDE)
    y = lax.div(docs, 2 * SIDE)

    def place(px, py, pcore):
        return (lax.rem(py + SIDE, SIDE) * SIDE + lax.rem(px, SIDE)) * 2 + lax.rem(pcore, 2)

    def plane(pz):
        return lax.rem(pz + PLANES, PLANES)

    def turn(py):
        return lax.div(lax.rem(py + 3, SIDE), 2)

    sibling = place(x, y, core + 1)
    ahead = place(x, y + 1, core + turn(y + 1))
    behind = place(x, y - 1, core)
    from_ahead = place(x, y + 1, core)
    from_behind = place(x, y - 1, core + turn(y))

    load = pltpu.make_async_copy(embeds_ref, rows, load_sem)
    load.start()

    barrier = pltpu.get_barrier_semaphore()

    def greet(device):
        pl.semaphore_signal(barrier, inc=1, device_id=device, device_id_type=MESH)

    for step in range(1, SIDE):
        greet((place(x + step, y, core), z))
    greet((from_ahead, z))
    greet((from_behind, z))
    greet((sibling, z))
    greet((docs, plane(z + 1)))
    greet((docs, plane(z - 1)))

    clusters = cluster_ref[...]

    def ranks(numbers):
        member = [jnp.where(clusters == number, 1.0, 0.0).astype(F32) for number in numbers]
        stacked = jnp.concatenate(member, axis=0).astype(BF16)
        before = jnp.where(iota((128, 128), 0) < iota((128, 128), 1), 1.0, 0.0).astype(BF16)
        within = jnp.dot(stacked, before, preferred_element_type=F32)
        totals = jnp.dot(stacked, jnp.ones((128, 128), BF16), preferred_element_type=F32)
        lines = len(member) * LINES
        above = (iota((lines, lines), 1) < iota((lines, lines), 0)) & (
            lax.div(iota((lines, lines), 1), LINES) == lax.div(iota((lines, lines), 0), LINES)
        )
        offsets = jnp.dot(
            jnp.where(above, 1.0, 0.0).astype(BF16), totals.astype(BF16), preferred_element_type=F32
        )
        return member, within + offsets, totals

    member, rank, totals = ranks([SIDE * z + b for b in range(4)])
    positions = [jnp.where(member[b] > 0, rank[b * LINES : (b + 1) * LINES], -1.0) for b in range(4)]
    counts = [jnp.sum(totals[b * LINES : (b + 1) * LINES], axis=0, keepdims=True) for b in range(4)]

    def mark_slots(low, high):
        size = high - low
        slot = iota((size, 128), 0).astype(F32) + low
        for b in range(4):
            for r in range(LINES):
                pick[b * size : (b + 1) * size, r * 128 : (r + 1) * 128] = jnp.where(
                    slot == positions[b][r : r + 1], 1.0, 0.0
                ).astype(BF16)

    def take_slots(low, high):
        size = high - low

        def gather(n, carry):
            cols = pl.ds(pl.multiple_of(n * 256, 256), 256)
            gathered[0 : 4 * size, cols] = jnp.dot(
                pick[0 : 4 * size, :], rows[:, cols], preferred_element_type=F32
            )
            return carry

        lax.fori_loop(0, WIDTH // 256, gather, 0)
        slot = iota((size, 128), 0).astype(F32) + low
        for b in range(4):
            values = gathered[b * size : (b + 1) * size, :]
            inverse = lax.rsqrt(jnp.sum(values * values, axis=1, keepdims=True) + EPSILON)
            scaled = values * inverse
            empty = (slot >= counts[b]) & (iota((size, 128), 1) == 0)
            head = jnp.where(empty, PADDED, scaled[:, 0:128]).astype(BF16)
            unit = scaled.astype(BF16)
            for part in range(0, size, PIECE):
                at = ((low + part) // PIECE * 4 + b) * PIECE
                blocks[at : at + PIECE, :] = unit[part : part + PIECE]
                blocks[at : at + PIECE, 0:128] = head[part : part + PIECE]

    mark_slots(0, EARLY)
    load.wait()
    take_slots(0, EARLY)
    pl.semaphore_wait(barrier, SIDE + 4)

    def piece(t, group, source):
        return members.at[pl.ds(pl.multiple_of(group * REGION + t * GROUP + source * PIECE, PIECE), PIECE)]

    def block(t, b):
        return blocks.at[pl.ds(pl.multiple_of((t * 4 + b) * PIECE, PIECE), PIECE)]

    def arrival(ref, sem):
        return pltpu.make_async_copy(ref, ref, sem)

    def ship(t, step):
        column = lax.rem(x + step, SIDE)
        return pltpu.make_async_remote_copy(
            src_ref=block(t, column), dst_ref=piece(t, OWN, x),
            send_sem=shipped.at[t, step], recv_sem=arrive.at[t, x],
            device_id=(place(column, y, core), z), device_id_type=MESH,
        )

    def pass_on(t, source, src, group):
        return pltpu.make_async_remote_copy(
            src_ref=src, dst_ref=piece(t, group, source),
            send_sem=passed.at[t, source, group - PREVIOUS], recv_sem=near_arrive.at[t, source, group - PREVIOUS],
            device_id=(behind if group == NEXT else ahead, z), device_id_type=MESH,
        )

    def pass_both(t, source, src):
        pass_on(t, source, src, NEXT).start()
        pass_on(t, source, src, PREVIOUS).start()

    def swap(t):
        return pltpu.make_async_remote_copy(
            src_ref=members.at[pl.ds(OWN * REGION + t * GROUP, GROUP)],
            dst_ref=members.at[pl.ds(OTHER * REGION + t * GROUP, GROUP)],
            send_sem=swap_sent.at[t], recv_sem=swap_arrive.at[t],
            device_id=(sibling, z), device_id_type=MESH,
        )

    def start_ships(t):
        for step in (2, 3, 1):
            ship(t, step).start()

    def end_ships(t):
        for step in (2, 3, 1):
            ship(t, step).wait_send()

    def keep(t):
        pass_both(t, x, block(t, x))
        pltpu.make_async_copy(block(t, x), piece(t, OWN, x), arrive.at[t, x]).start()

    def relay(t):
        for step in (3, 1, 2):
            source = lax.rem(x + step, SIDE)
            arrival(piece(t, OWN, source), arrive.at[t, source]).wait()
            pass_both(t, source, piece(t, OWN, source))
        arrival(piece(t, OWN, x), arrive.at[t, x]).wait()
        swap(t).start()

    def await_near(t):
        for source in range(SIDE):
            for group in (NEXT, PREVIOUS):
                arrival(piece(t, group, source), near_arrive.at[t, source, group - PREVIOUS]).wait()

    def tell(step):
        for way in (1, -1):
            pl.semaphore_signal(hello.at[step], inc=1, device_id=(docs, plane(z + way)), device_id_type=MESH)

    def mark(start, size):
        chosen = jnp.where((iota((16, 128), 0) < 8) & (iota((16, 128), 1) == 0), 1.0, 0.0).astype(BF16)
        heads = lax.dot_general(chosen, members[start : start + size, 0:128], NT, preferred_element_type=F32)
        col_bias[:, start : start + size] = jnp.where(heads[0:8] > 1.5, FAR, 0.0)

    def bias_of_rows(start, size):
        first = members[start : start + size, 0:128].astype(F32)[:, 0:1]
        return jnp.where(first > 1.5, FAR, 0.0)

    def scores(base, size, start, width):
        return lax.dot_general(
            members[base : base + size, :], members[start : start + width, :], NT, preferred_element_type=F32
        )

    def along_rows(best, score, start, width):
        biased = score + col_bias[0:1, start : start + width]
        for c in range(0, width, 128):
            best = jnp.maximum(best, biased[:, c : c + 128])
        return best

    def turned(best):
        return jnp.max(best.T, axis=0, keepdims=True)

    def pair_own():
        row_max[...] = jnp.full((REGION, 128), LOWEST, F32)
        for n in range(2 * REGION // 256):
            start = n * 256
            mark(start, 256)
            score = scores(0, REGION, start, 256)
            if start < REGION:
                score = jnp.where(iota((REGION, 256), 0) == iota((REGION, 256), 1) + start, LOWEST, score)
            row_max[...] = along_rows(row_max[...], score, start, 256)
        for t in range(STAGES):
            answer[OWN, t : t + 1] = turned(row_max[t * GROUP : (t + 1) * GROUP, :])

    def pair(base, start, stop):
        bias = bias_of_rows(base, GROUP)
        best = jnp.full((GROUP, 128), LOWEST, F32)
        while start < stop:
            width = min(512, stop - start)
            score = scores(base, GROUP, start, width)
            best = along_rows(best, score, start, width)
            biased = (score + bias).reshape(GROUP // 8, 8, width)
            span = slice(start, start + width)
            col_max[:, span] = jnp.maximum(col_max[:, span], jnp.max(biased, axis=0))
            start += width
        return turned(best)

    def pair_near(t):
        nexts, previous = NEXT * REGION + t * GROUP, PREVIOUS * REGION + t * GROUP
        mark(previous, GROUP)
        answer[NEXT, t : t + 1] = pair(nexts, 0, previous + GROUP)
        if t:
            answer[PREVIOUS, t : t + 1] = pair(previous, NEXT * REGION, nexts)
        if t + 1 < STAGES:
            mark(nexts, GROUP)

    def hear(step):
        pl.semaphore_wait(hello.at[step], 2)

    start_ships(0)
    keep(0)
    tell(0)
    mark_slots(EARLY, SLOTS)
    take_slots(EARLY, SLOTS)
    start_ships(1)
    for t in range(1, STAGES):
        keep(t)
    col_max[...] = jnp.full(col_max.shape, LOWEST, F32)
    answer[...] = jnp.full(answer.shape, LOWEST, F32)
    for t in range(STAGES):
        relay(t)
        end_ships(t)
        if t + 2 < STAGES:
            start_ships(t + 2)
        hear(t)
        if t + 1 < STAGES:
            tell(t + 1)
        if t == 0:
            everyone, place_in, _ = ranks(list(range(CLUSTERS)))
            own_rank = jnp.zeros((LINES, 128), F32)
            for number, mask in enumerate(everyone):
                own_rank = own_rank + mask * place_in[number * LINES : (number + 1) * LINES]
            rank_of[...] = own_rank

    for t in range(STAGES):
        swap(t).wait_recv()
    pair_own()
    for t in range(STAGES):
        await_near(t)
        pair_near(t)

    for group in (NEXT, PREVIOUS, OTHER, OWN):
        for t in range(STAGES):
            start = group * REGION + t * GROUP
            best = jnp.max(col_max[:, start : start + GROUP], axis=0, keepdims=True)
            answer[group, t : t + 1] = jnp.maximum(answer[group, t : t + 1], best)

    def give(group):
        device = {OTHER: sibling, NEXT: from_ahead, PREVIOUS: from_behind}[group]
        return pltpu.make_async_remote_copy(
            src_ref=answer.at[group], dst_ref=near.at[group], send_sem=near_sent.at[group],
            recv_sem=back_near.at[group], device_id=(device, z), device_id_type=MESH,
        )

    for group in (NEXT, PREVIOUS, OTHER):
        give(group).start()
    best = answer[OWN]
    for group in (OTHER, NEXT, PREVIOUS):
        arrival(near.at[group], back_near.at[group]).wait()
        best = jnp.maximum(best, near[group])
    block_of = lax.div(iota((8, 128), 1), PIECE)
    moved = {by: pltpu.roll(best, by * PIECE % 128, 1) for by in range(1 - SIDE, STAGES)}
    for source in range(SIDE):
        spaced = jnp.zeros((8, 128), F32)
        for t in range(STAGES):
            spaced = jnp.where((iota((8, 128), 0) == t) & (block_of == t), moved[t - source], spaced)
        final[source] = jnp.sum(spaced, axis=0, keepdims=True)

    number = SIDE * z + x

    def spread(step, up):
        column = lax.rem(x + step, SIDE)
        return pltpu.make_async_remote_copy(
            src_ref=final.at[column], dst_ref=returned.at[number], send_sem=back_sent.at[up, step],
            recv_sem=back_arrive, device_id=(place(column, y, core), plane(z + up)), device_id_type=MESH,
        )

    spreads = [spread(step, up) for up in (4, 3, 5, 2, 6, 1, 7, 0) for step in (2, 1, 3, 0) if step or up]
    for copy in spreads:
        copy.start()
    pltpu.make_async_copy(final.at[x], returned.at[number], back_arrive).start()
    pltpu.make_async_copy(returned, returned, back_arrive).wait()

    found = returned[...].reshape(CLUSTERS, 128)
    high = found.astype(BF16)
    rest = found - high.astype(F32)
    middle = rest.astype(BF16)
    low = (rest - middle.astype(F32)).astype(BF16)
    parts = jnp.concatenate([high, middle, low], axis=0)
    slot = iota((128, 128), 0).astype(F32)
    line = iota((CLUSTERS, 128), 0)
    for r in range(LINES):
        chosen = jnp.where(slot == rank_of[r : r + 1, :], 1.0, 0.0).astype(BF16)
        taken = jnp.dot(parts, chosen, preferred_element_type=F32)
        taken = taken[0:CLUSTERS] + taken[CLUSTERS : 2 * CLUSTERS] + taken[2 * CLUSTERS :]
        out_ref[r : r + 1] = jnp.sum(
            jnp.where(line == cluster_ref[r : r + 1, :], taken, 0.0), axis=0, keepdims=True
        )

    for group in (OTHER, NEXT, PREVIOUS):
        give(group).wait_send()
    for copy in spreads:
        copy.wait_send()

    def end_stage(t, carry):
        swap(t).wait_send()
        for source in range(SIDE):
            for group in (NEXT, PREVIOUS):
                pass_on(t, source, piece(t, OWN, source), group).wait_send()
        return carry

    lax.fori_loop(0, STAGES, end_stage, 0)


def local(embeds, cluster_of):
    dma = pltpu.SemaphoreType.DMA
    out = pl.pallas_call(
        kernel,
        out_shape=jax.ShapeDtypeStruct((LINES, 128), F32),
        in_specs=[pl.BlockSpec(memory_space=pltpu.VMEM), pl.BlockSpec(memory_space=pl.ANY)],
        out_specs=pl.BlockSpec(memory_space=pltpu.VMEM),
        scratch_shapes=[
            pltpu.VMEM((DOCS, WIDTH), BF16),
            pltpu.VMEM((4 * (SLOTS - EARLY), DOCS), BF16),
            pltpu.VMEM((4 * (SLOTS - EARLY), WIDTH), F32),
            pltpu.VMEM((4 * SLOTS, WIDTH), BF16),
            pltpu.VMEM((MEMBERS, WIDTH), BF16),
            pltpu.VMEM((8, MEMBERS), F32),
            pltpu.VMEM((REGION, 128), F32),
            pltpu.VMEM((8, MEMBERS), F32),
            pltpu.VMEM((4, 8, 128), F32),
            pltpu.VMEM((4, 8, 128), F32),
            pltpu.VMEM((SIDE, 1, 128), F32),
            pltpu.VMEM((CLUSTERS, 1, 128), F32),
            pltpu.VMEM((LINES, 128), F32),
            dma,
            dma((STAGES, SIDE)),
            dma((STAGES, SIDE)),
            dma((STAGES, SIDE, 2)),
            dma((STAGES, SIDE, 2)),
            dma((STAGES,)),
            dma((STAGES,)),
            dma((4,)),
            dma((4,)),
            dma((PLANES, SIDE)),
            dma,
            pltpu.SemaphoreType.REGULAR((STAGES,)),
        ],
        compiler_params=pltpu.CompilerParams(
            collective_id=0, has_side_effects=True, vmem_limit_bytes=48 * 2**20
        ),
        cost_estimate=pl.CostEstimate(flops=8 * 10**9, bytes_accessed=4 * 2**20, transcendentals=512),
    )(cluster_of.reshape(LINES, 128), embeds)
    return out.reshape(DOCS)


def solution(mesh):
    return jax.shard_map(
        local,
        mesh=mesh,
        in_specs=(P("docs", None), P("docs")),
        out_specs=P("docs"),
        check_vma=False,
    )
```

time: 56.9 us -> 50.3 us (0.88)
  Pallas kernels: 53.3 us -> 46.6 us
    pallas_call x1, Pallas kernels: 53.3 us -> 46.6 us  [local(): pl.pallas_call(kernel, out_shape=jax.ShapeDtypeStruct((LINES, 128), F32),...]
where the time goes in v3:
time: 50.3 us; the launch traced here: 50.1 us
  Pallas kernels  46.6 us (93%)
  local copies, waits for them, and re-layouts  3.48 us (7%)
    pallas_call x1, Pallas kernels, local(): pl.pallas_call(kernel, out_shape=jax.ShapeDtypeStruct((LINES, 128), F32),...  46.6 us
    unnamed x5, local copies, waits for them, and re-layouts  3.48 us

profile of v3, /device:TPU:1, one launch (start us, length us, event | category | flops | bytes accessed | tf_op | source)
XLA Modules:
  0.0 50.1 jit_solution(3733779149290579183)
XLA Ops:
  0.0 0.0 copy-start
  0.0 2.2 %copy-done = bf16[2048,1024]{1,0:T(8,128)(2,1)S(1)} copy-done((bf16[2048,1024]{1,0:T(8,128)(2,1)S(1)}, bf16[2048,1024]{1,0:T(8,128)(2,1)}, u32[]{:S(2)}) %copy-start) | copy-done | bytes 4194328
  2.2 0.0 copy-start.1
  2.2 0.7 %copy-done.1 = s32[2048]{0:T(1024)S(1)} copy-done((s32[2048]{0:T(1024)S(1)}, s32[2048]{0:T(1024)}, u32[]{:S(2)}) %copy-start.1) | copy-done | bytes 8216
  2.9 46.6 %shard_map.28 = f32[16,128]{1,0:T(8,128)S(1)} custom-call(s32[16,128]{1,0:T(8,128)S(1)} %bitcast.3, bf16[2048,1024]{1,0:T(8,128)(2,1)S(1)} %copy-done), custom_call_target="tpu_custom_call" | custom-call | flops 8000000000 | bytes 4194304 | tf_op jit(solution)/shard_map/pallas_call | solution.py:374
  49.5 0.6 %copy.4 = f32[2048]{0:T(1024)} copy(f32[2048]{0:T(1024)S(1)} %bitcast.2) | data formatting | bytes 16384
Async XLA Ops:
  0.0 2.2 %copy-start = (bf16[2048,1024]{1,0:T(8,128)(2,1)S(1)}, bf16[2048,1024]{1,0:T(8,128)(2,1)}, u32[]{:S(2)}) copy-start(bf16[2048,1024]{1,0:T(8,128)(2,1)} %embeds_ref.1) | copy-start | bytes 12582916
  2.2 0.7 %copy-start.1 = (s32[2048]{0:T(1024)S(1)}, s32[2048]{0:T(1024)}, u32[]{:S(2)}) copy-start(s32[2048]{0:T(1024)} %param.3) | copy-start | bytes 24580

commit v4 on v3

--- a/solution.py
+++ b/solution.py
@@ -22,7 +22,7 @@
 GROUP = SIDE * PIECE
 REGION = STAGES * GROUP
 MEMBERS = 4 * REGION
-EARLY = PIECE
+LOADS = 8
 LINES = DOCS // 128
 OWN, OTHER, PREVIOUS, NEXT = range(4)
 
@@ -37,10 +37,10 @@
 
 
 def kernel(
-    cluster_ref, embeds_ref, out_ref,
-    rows, pick, gathered, blocks, members, col_bias, row_max, col_max, answer,
+    cluster_hbm, embeds_ref, out_ref,
+    cluster_ref, rows, pick, gathered, blocks, members, col_bias, row_max, col_max, answer,
     near, final, returned, rank_of,
-    load_sem, shipped, arrive, passed, near_arrive, swap_sent, swap_arrive, near_sent, back_near, back_sent,
+    cluster_sem, load_sem, shipped, arrive, passed, near_arrive, swap_sent, swap_arrive, near_sent, back_near, back_sent,
     back_arrive, hello,
 ):
     docs = lax.axis_index("docs")
@@ -64,8 +64,13 @@
     from_ahead = place(x, y + 1, core)
     from_behind = place(x, y - 1, core + turn(y))
 
-    load = pltpu.make_async_copy(embeds_ref, rows, load_sem)
-    load.start()
+    cluster_load = pltpu.make_async_copy(cluster_hbm, cluster_ref, cluster_sem)
+    cluster_load.start()
+    loads = []
+    for part in range(LOADS):
+        span = pl.ds(part * (DOCS // LOADS), DOCS // LOADS)
+        loads.append(pltpu.make_async_copy(embeds_ref.at[span], rows.at[span], load_sem.at[part]))
+        loads[-1].start()
 
     barrier = pltpu.get_barrier_semaphore()
 
@@ -80,6 +85,7 @@
     greet((docs, plane(z + 1)))
     greet((docs, plane(z - 1)))
 
+    cluster_load.wait()
     clusters = cluster_ref[...]
 
     def ranks(numbers):
@@ -101,42 +107,44 @@
     positions = [jnp.where(member[b] > 0, rank[b * LINES : (b + 1) * LINES], -1.0) for b in range(4)]
     counts = [jnp.sum(totals[b * LINES : (b + 1) * LINES], axis=0, keepdims=True) for b in range(4)]
 
-    def mark_slots(low, high):
-        size = high - low
-        slot = iota((size, 128), 0).astype(F32) + low
+    def mark_slots(t):
+        slot = iota((PIECE, 128), 0).astype(F32) + t * PIECE
         for b in range(4):
             for r in range(LINES):
-                pick[b * size : (b + 1) * size, r * 128 : (r + 1) * 128] = jnp.where(
+                pick[b * PIECE : (b + 1) * PIECE, r * 128 : (r + 1) * 128] = jnp.where(
                     slot == positions[b][r : r + 1], 1.0, 0.0
                 ).astype(BF16)
 
-    def take_slots(low, high):
-        size = high - low
-
+    def scale_slots(t):
+        slot = iota((PIECE, 128), 0).astype(F32) + t * PIECE
+        for b in range(4):
+            values = gathered[b * PIECE : (b + 1) * PIECE, :]
+            inverse = lax.rsqrt(jnp.sum(values * values, axis=1, keepdims=True) + EPSILON)
+            scaled = values * inverse
+            empty = (slot >= counts[b]) & (iota((PIECE, 128), 1) == 0)
+            at = (t * 4 + b) * PIECE
+            blocks[at : at + PIECE, :] = scaled.astype(BF16)
+            blocks[at : at + PIECE, 0:128] = jnp.where(empty, PADDED, scaled[:, 0:128]).astype(BF16)
+
+    def gather_part(part):
+        span = slice(part * (DOCS // LOADS), (part + 1) * (DOCS // LOADS))
+        for c in range(0, WIDTH, 256):
+            taken = jnp.dot(pick[:, span], rows[span, c : c + 256], preferred_element_type=F32)
+            gathered[:, c : c + 256] = taken if part == 0 else gathered[:, c : c + 256] + taken
+
+    def gather_all():
         def gather(n, carry):
             cols = pl.ds(pl.multiple_of(n * 256, 256), 256)
-            gathered[0 : 4 * size, cols] = jnp.dot(
-                pick[0 : 4 * size, :], rows[:, cols], preferred_element_type=F32
-            )
+            gathered[:, cols] = jnp.dot(pick[...], rows[:, cols], preferred_element_type=F32)
             return carry
 
         lax.fori_loop(0, WIDTH // 256, gather, 0)
-        slot = iota((size, 128), 0).astype(F32) + low
-        for b in range(4):
-            values = gathered[b * size : (b + 1) * size, :]
-            inverse = lax.rsqrt(jnp.sum(values * values, axis=1, keepdims=True) + EPSILON)
-            scaled = values * inverse
-            empty = (slot >= counts[b]) & (iota((size, 128), 1) == 0)
-            head = jnp.where(empty, PADDED, scaled[:, 0:128]).astype(BF16)
-            unit = scaled.astype(BF16)
-            for part in range(0, size, PIECE):
-                at = ((low + part) // PIECE * 4 + b) * PIECE
-                blocks[at : at + PIECE, :] = unit[part : part + PIECE]
-                blocks[at : at + PIECE, 0:128] = head[part : part + PIECE]
-
-    mark_slots(0, EARLY)
-    load.wait()
-    take_slots(0, EARLY)
+
+    mark_slots(0)
+    for part in range(LOADS):
+        loads[part].wait()
+        gather_part(part)
+    scale_slots(0)
     pl.semaphore_wait(barrier, SIDE + 4)
 
     def piece(t, group, source):
@@ -267,11 +275,13 @@
     start_ships(0)
     keep(0)
     tell(0)
-    mark_slots(EARLY, SLOTS)
-    take_slots(EARLY, SLOTS)
-    start_ships(1)
     for t in range(1, STAGES):
+        mark_slots(t)
+        gather_all()
+        scale_slots(t)
         keep(t)
+        if t == 1:
+            start_ships(t)
     col_max[...] = jnp.full(col_max.shape, LOWEST, F32)
     answer[...] = jnp.full(answer.shape, LOWEST, F32)
     for t in range(STAGES):
@@ -336,6 +346,20 @@
     for copy in spreads:
         copy.start()
     pltpu.make_async_copy(final.at[x], returned.at[number], back_arrive).start()
+
+    for group in (OTHER, NEXT, PREVIOUS):
+        give(group).wait_send()
+
+    def end_stage(t, carry):
+        swap(t).wait_send()
+        for source in range(SIDE):
+            for group in (NEXT, PREVIOUS):
+                pass_on(t, source, piece(t, OWN, source), group).wait_send()
+        return carry
+
+    lax.fori_loop(0, STAGES, end_stage, 0)
+    for copy in spreads:
+        copy.wait_send()
     pltpu.make_async_copy(returned, returned, back_arrive).wait()
 
     found = returned[...].reshape(CLUSTERS, 128)
@@ -354,32 +378,19 @@
             jnp.where(line == cluster_ref[r : r + 1, :], taken, 0.0), axis=0, keepdims=True
         )
 
-    for group in (OTHER, NEXT, PREVIOUS):
-        give(group).wait_send()
-    for copy in spreads:
-        copy.wait_send()
-
-    def end_stage(t, carry):
-        swap(t).wait_send()
-        for source in range(SIDE):
-            for group in (NEXT, PREVIOUS):
-                pass_on(t, source, piece(t, OWN, source), group).wait_send()
-        return carry
-
-    lax.fori_loop(0, STAGES, end_stage, 0)
-
 
 def local(embeds, cluster_of):
     dma = pltpu.SemaphoreType.DMA
     out = pl.pallas_call(
         kernel,
         out_shape=jax.ShapeDtypeStruct((LINES, 128), F32),
-        in_specs=[pl.BlockSpec(memory_space=pltpu.VMEM), pl.BlockSpec(memory_space=pl.ANY)],
+        in_specs=[pl.BlockSpec(memory_space=pl.ANY)] * 2,
         out_specs=pl.BlockSpec(memory_space=pltpu.VMEM),
         scratch_shapes=[
+            pltpu.VMEM((LINES, 128), jnp.int32),
             pltpu.VMEM((DOCS, WIDTH), BF16),
-            pltpu.VMEM((4 * (SLOTS - EARLY), DOCS), BF16),
-            pltpu.VMEM((4 * (SLOTS - EARLY), WIDTH), F32),
+            pltpu.VMEM((GROUP, DOCS), BF16),
+            pltpu.VMEM((GROUP, WIDTH), F32),
             pltpu.VMEM((4 * SLOTS, WIDTH), BF16),
             pltpu.VMEM((MEMBERS, WIDTH), BF16),
             pltpu.VMEM((8, MEMBERS), F32),
@@ -391,6 +402,7 @@
             pltpu.VMEM((CLUSTERS, 1, 128), F32),
             pltpu.VMEM((LINES, 128), F32),
             dma,
+            dma((LOADS,)),
             dma((STAGES, SIDE)),
             dma((STAGES, SIDE)),
             dma((STAGES, SIDE, 2)),
@@ -404,7 +416,7 @@
             pltpu.SemaphoreType.REGULAR((STAGES,)),
         ],
         compiler_params=pltpu.CompilerParams(
-            collective_id=0, has_side_effects=True, vmem_limit_bytes=48 * 2**20
+            collective_id=0, has_side_effects=True, vmem_limit_bytes=53 * 2**20
         ),
         cost_estimate=pl.CostEstimate(flops=8 * 10**9, bytes_accessed=4 * 2**20, transcendentals=512),
     )(cluster_of.reshape(LINES, 128), embeds)

time: 50.3 us -> 47.3 us (0.940)
  local copies, waits for them, and re-layouts: 3.48 us -> 1.3 us
  Pallas kernels: 46.6 us -> 45.8 us
    unnamed x5 -> x3, local copies, waits for them, and re-layouts: 3.48 us -> 1.3 us
    pallas_call x1, Pallas kernels: 46.6 us -> 45.8 us  [local(): pl.pallas_call(kernel, out_shape=jax.ShapeDtypeStruct((LINES, 128), F32),...]
where the time goes in v4:
time: 47.3 us; the launch traced here: 47.1 us
  Pallas kernels  45.8 us (97%)
  local copies, waits for them, and re-layouts  1.3 us (3%)
    pallas_call x1, Pallas kernels, local(): pl.pallas_call(kernel, out_shape=jax.ShapeDtypeStruct((LINES, 128), F32),...  45.8 us
    unnamed x3, local copies, waits for them, and re-layouts  1.3 us

profile of v4, /device:TPU:1, one launch (start us, length us, event | category | flops | bytes accessed | tf_op | source)
XLA Modules:
  0.0 47.1 jit_solution(7960063676534083843)
XLA Ops:
  0.0 0.0 copy-start
  0.0 0.7 %copy-done = s32[2048]{0:T(1024)S(1)} copy-done((s32[2048]{0:T(1024)S(1)}, s32[2048]{0:T(1024)}, u32[]{:S(2)}) %copy-start) | copy-done | bytes 8216
  0.7 45.8 %shard_map.28 = f32[16,128]{1,0:T(8,128)S(1)} custom-call(s32[16,128]{1,0:T(8,128)S(1)} %bitcast.3, bf16[2048,1024]{1,0:T(8,128)(2,1)} %embeds_ref.1), custom_call_target="tpu_custom_call" | custom-call | flops 8000000000 | bytes 4194304 | tf_op jit(solution)/shard_map/pallas_call | solution.py:384
  46.5 0.6 %copy.4 = f32[2048]{0:T(1024)} copy(f32[2048]{0:T(1024)S(1)} %bitcast.2) | data formatting | bytes 16384
Async XLA Ops:
  0.0 0.7 %copy-start = (s32[2048]{0:T(1024)S(1)}, s32[2048]{0:T(1024)}, u32[]{:S(2)}) copy-start(s32[2048]{0:T(1024)} %param.3) | copy-start | bytes 24580

commit v5 on v4

--- a/solution.py
+++ b/solution.py
@@ -23,8 +23,10 @@
 REGION = STAGES * GROUP
 MEMBERS = 4 * REGION
 LOADS = 8
+DETOURS = (0, 1)
+FAR_SOURCE = 3
 LINES = DOCS // 128
-OWN, OTHER, PREVIOUS, NEXT = range(4)
+OWN, OTHER, Y_PART, X_PART = range(4)
 
 MESH = pl.DeviceIdType.MESH
 F32 = jnp.float32
@@ -39,9 +41,9 @@
 def kernel(
     cluster_hbm, embeds_ref, out_ref,
     cluster_ref, rows, pick, gathered, blocks, members, col_bias, row_max, col_max, answer,
-    near, final, returned, rank_of,
+    near, final, returned, rank_of, detours,
     cluster_sem, load_sem, shipped, arrive, passed, near_arrive, swap_sent, swap_arrive, near_sent, back_near, back_sent,
-    back_arrive, hello,
+    back_arrive, hello, detour_sent, detour_arrive, detour_passed,
 ):
     docs = lax.axis_index("docs")
     z = lax.axis_index("grp")
@@ -50,19 +52,29 @@
     y = lax.div(docs, 2 * SIDE)
 
     def place(px, py, pcore):
-        return (lax.rem(py + SIDE, SIDE) * SIDE + lax.rem(px, SIDE)) * 2 + lax.rem(pcore, 2)
+        return (lax.rem(py + SIDE, SIDE) * SIDE + lax.rem(px + SIDE, SIDE)) * 2 + lax.rem(pcore, 2)
 
     def plane(pz):
         return lax.rem(pz + PLANES, PLANES)
 
-    def turn(py):
-        return lax.div(lax.rem(py + 3, SIDE), 2)
+    shifted = lax.rem(z, 2)
+    odd_x = lax.rem(x + shifted, 2)
+    odd_y = lax.rem(y + shifted, 2)
+    in_x, out_x = x + 1 - 2 * odd_x, x - 1 + 2 * odd_x
+    in_y, out_y = y + 1 - 2 * odd_y, y - 1 + 2 * odd_y
+
+    def cluster_at(px, py):
+        tile_x = lax.div(lax.rem(px + SIDE - shifted, SIDE), 2)
+        tile_y = lax.div(lax.rem(py + SIDE - shifted, SIDE), 2)
+        return SIDE * z + 2 * tile_y + tile_x
+
+    chips = [(x, y), (out_x, y), (x, out_y), (out_x, out_y)]
+    numbers = [cluster_at(px + SIDE, py + SIDE) for px, py in chips]
 
     sibling = place(x, y, core + 1)
-    ahead = place(x, y + 1, core + turn(y + 1))
-    behind = place(x, y - 1, core)
-    from_ahead = place(x, y + 1, core)
-    from_behind = place(x, y - 1, core + turn(y))
+    to_x = place(in_x, y, core)
+    to_y = place(x, in_y, core + 1 - odd_y)
+    from_y = place(x, in_y, core + odd_y)
 
     cluster_load = pltpu.make_async_copy(cluster_hbm, cluster_ref, cluster_sem)
     cluster_load.start()
@@ -77,13 +89,17 @@
     def greet(device):
         pl.semaphore_signal(barrier, inc=1, device_id=device, device_id_type=MESH)
 
-    for step in range(1, SIDE):
-        greet((place(x + step, y, core), z))
-    greet((from_ahead, z))
-    greet((from_behind, z))
+    for dx in (-1, 0, 1):
+        for dy in (-1, 0, 1):
+            if dx or dy:
+                greet((place(x + dx, y + dy, core), z))
+    greet((place(x, y + 1, core + 1), z))
+    greet((place(x, y - 1, core + 1), z))
     greet((sibling, z))
     greet((docs, plane(z + 1)))
     greet((docs, plane(z - 1)))
+    greet((place(out_x, y, core), plane(z - 1)))
+    greet((place(x, out_y, core + 1 - odd_y), plane(z + 1)))
 
     cluster_load.wait()
     clusters = cluster_ref[...]
@@ -103,7 +119,7 @@
         )
         return member, within + offsets, totals
 
-    member, rank, totals = ranks([SIDE * z + b for b in range(4)])
+    member, rank, totals = ranks(numbers)
     positions = [jnp.where(member[b] > 0, rank[b * LINES : (b + 1) * LINES], -1.0) for b in range(4)]
     counts = [jnp.sum(totals[b * LINES : (b + 1) * LINES], axis=0, keepdims=True) for b in range(4)]
 
@@ -145,7 +161,7 @@
         loads[part].wait()
         gather_part(part)
     scale_slots(0)
-    pl.semaphore_wait(barrier, SIDE + 4)
+    pl.semaphore_wait(barrier, 15)
 
     def piece(t, group, source):
         return members.at[pl.ds(pl.multiple_of(group * REGION + t * GROUP + source * PIECE, PIECE), PIECE)]
@@ -156,24 +172,44 @@
     def arrival(ref, sem):
         return pltpu.make_async_copy(ref, ref, sem)
 
-    def ship(t, step):
-        column = lax.rem(x + step, SIDE)
-        return pltpu.make_async_remote_copy(
-            src_ref=block(t, column), dst_ref=piece(t, OWN, x),
-            send_sem=shipped.at[t, step], recv_sem=arrive.at[t, x],
-            device_id=(place(column, y, core), z), device_id_type=MESH,
+    def ship(t, b):
+        return pltpu.make_async_remote_copy(
+            src_ref=block(t, b), dst_ref=piece(t, OWN, b), send_sem=shipped.at[t, b], recv_sem=arrive.at[t, b],
+            device_id=(place(*chips[b], core), z), device_id_type=MESH,
         )
 
     def pass_on(t, source, src, group):
         return pltpu.make_async_remote_copy(
             src_ref=src, dst_ref=piece(t, group, source),
-            send_sem=passed.at[t, source, group - PREVIOUS], recv_sem=near_arrive.at[t, source, group - PREVIOUS],
-            device_id=(behind if group == NEXT else ahead, z), device_id_type=MESH,
+            send_sem=passed.at[t, source, group - Y_PART], recv_sem=near_arrive.at[t, source, group - Y_PART],
+            device_id=(to_x if group == X_PART else to_y, z), device_id_type=MESH,
         )
 
     def pass_both(t, source, src):
-        pass_on(t, source, src, NEXT).start()
-        pass_on(t, source, src, PREVIOUS).start()
+        pass_on(t, source, src, X_PART).start()
+        pass_on(t, source, src, Y_PART).start()
+
+    def detour(t, group):
+        way = group - Y_PART
+        return pltpu.make_async_remote_copy(
+            src_ref=piece(t, OWN, FAR_SOURCE), dst_ref=detours.at[way, t],
+            send_sem=detour_sent.at[way, t], recv_sem=detour_arrive.at[way, t],
+            device_id=(to_x, plane(z + 1)) if group == X_PART else (to_y, plane(z - 1)), device_id_type=MESH,
+        )
+
+    def pass_detour(t, group):
+        way = group - Y_PART
+        return pltpu.make_async_remote_copy(
+            src_ref=detours.at[way, t], dst_ref=piece(t, group, FAR_SOURCE),
+            send_sem=detour_passed.at[way, t], recv_sem=near_arrive.at[t, FAR_SOURCE, way],
+            device_id=(docs, plane(z - 1) if group == X_PART else plane(z + 1)), device_id_type=MESH,
+        )
+
+    def pass_detours(t):
+        for group in (X_PART, Y_PART):
+            way = group - Y_PART
+            arrival(detours.at[way, t], detour_arrive.at[way, t]).wait()
+            pass_detour(t, group).start()
 
     def swap(t):
         return pltpu.make_async_remote_copy(
@@ -184,29 +220,32 @@
         )
 
     def start_ships(t):
-        for step in (2, 3, 1):
-            ship(t, step).start()
+        for b in (3, 1, 2):
+            ship(t, b).start()
 
     def end_ships(t):
-        for step in (2, 3, 1):
-            ship(t, step).wait_send()
+        for b in (3, 1, 2):
+            ship(t, b).wait_send()
 
     def keep(t):
-        pass_both(t, x, block(t, x))
-        pltpu.make_async_copy(block(t, x), piece(t, OWN, x), arrive.at[t, x]).start()
+        pass_both(t, 0, block(t, 0))
+        pltpu.make_async_copy(block(t, 0), piece(t, OWN, 0), arrive.at[t, 0]).start()
 
     def relay(t):
-        for step in (3, 1, 2):
-            source = lax.rem(x + step, SIDE)
+        for source in (1, 2, 3):
             arrival(piece(t, OWN, source), arrive.at[t, source]).wait()
-            pass_both(t, source, piece(t, OWN, source))
-        arrival(piece(t, OWN, x), arrive.at[t, x]).wait()
+            if source == FAR_SOURCE and t in DETOURS:
+                detour(t, X_PART).start()
+                detour(t, Y_PART).start()
+            else:
+                pass_both(t, source, piece(t, OWN, source))
+        arrival(piece(t, OWN, 0), arrive.at[t, 0]).wait()
         swap(t).start()
 
     def await_near(t):
         for source in range(SIDE):
-            for group in (NEXT, PREVIOUS):
-                arrival(piece(t, group, source), near_arrive.at[t, source, group - PREVIOUS]).wait()
+            for group in (X_PART, Y_PART):
+                arrival(piece(t, group, source), near_arrive.at[t, source, group - Y_PART]).wait()
 
     def tell(step):
         for way in (1, -1):
@@ -247,27 +286,33 @@
         for t in range(STAGES):
             answer[OWN, t : t + 1] = turned(row_max[t * GROUP : (t + 1) * GROUP, :])
 
-    def pair(base, start, stop):
+    def pair(base, spans):
         bias = bias_of_rows(base, GROUP)
         best = jnp.full((GROUP, 128), LOWEST, F32)
-        while start < stop:
-            width = min(512, stop - start)
-            score = scores(base, GROUP, start, width)
-            best = along_rows(best, score, start, width)
+        for start, width in spans:
+            span = pl.ds(start, width)
+            score = lax.dot_general(
+                members[base : base + GROUP, :], members[span, :], NT, preferred_element_type=F32
+            )
+            biased = score + col_bias[0:1, span]
+            for c in range(0, width, 128):
+                best = jnp.maximum(best, biased[:, c : c + 128])
             biased = (score + bias).reshape(GROUP // 8, 8, width)
-            span = slice(start, start + width)
             col_max[:, span] = jnp.maximum(col_max[:, span], jnp.max(biased, axis=0))
-            start += width
         return turned(best)
 
+    facing = pl.multiple_of(odd_x * REGION, REGION)
+
     def pair_near(t):
-        nexts, previous = NEXT * REGION + t * GROUP, PREVIOUS * REGION + t * GROUP
-        mark(previous, GROUP)
-        answer[NEXT, t : t + 1] = pair(nexts, 0, previous + GROUP)
+        to_pair_x, to_pair_y = X_PART * REGION + t * GROUP, Y_PART * REGION + t * GROUP
+        mark(to_pair_y, GROUP)
+        answer[X_PART, t : t + 1] = pair(to_pair_x, [(facing, REGION), (Y_PART * REGION, (t + 1) * GROUP)])
+        spans = [(OWN * REGION, REGION)]
         if t:
-            answer[PREVIOUS, t : t + 1] = pair(previous, NEXT * REGION, nexts)
+            spans.append((X_PART * REGION, t * GROUP))
+        answer[Y_PART, t : t + 1] = pair(to_pair_y, spans)
         if t + 1 < STAGES:
-            mark(nexts, GROUP)
+            mark(to_pair_x, GROUP)
 
     def hear(step):
         pl.semaphore_wait(hello.at[step], 2)
@@ -279,16 +324,17 @@
         mark_slots(t)
         gather_all()
         scale_slots(t)
+        if t in (1, 3):
+            start_ships((t + 1) // 2)
         keep(t)
-        if t == 1:
-            start_ships(t)
     col_max[...] = jnp.full(col_max.shape, LOWEST, F32)
     answer[...] = jnp.full(answer.shape, LOWEST, F32)
     for t in range(STAGES):
         relay(t)
-        end_ships(t)
-        if t + 2 < STAGES:
-            start_ships(t + 2)
+        if t == 1:
+            start_ships(3)
+        if t - 1 in DETOURS:
+            pass_detours(t - 1)
         hear(t)
         if t + 1 < STAGES:
             tell(t + 1)
@@ -306,23 +352,23 @@
         await_near(t)
         pair_near(t)
 
-    for group in (NEXT, PREVIOUS, OTHER, OWN):
+    for group in (X_PART, Y_PART, OTHER, OWN):
         for t in range(STAGES):
             start = group * REGION + t * GROUP
             best = jnp.max(col_max[:, start : start + GROUP], axis=0, keepdims=True)
             answer[group, t : t + 1] = jnp.maximum(answer[group, t : t + 1], best)
 
     def give(group):
-        device = {OTHER: sibling, NEXT: from_ahead, PREVIOUS: from_behind}[group]
+        device = {OTHER: sibling, X_PART: to_x, Y_PART: from_y}[group]
         return pltpu.make_async_remote_copy(
             src_ref=answer.at[group], dst_ref=near.at[group], send_sem=near_sent.at[group],
             recv_sem=back_near.at[group], device_id=(device, z), device_id_type=MESH,
         )
 
-    for group in (NEXT, PREVIOUS, OTHER):
+    for group in (X_PART, Y_PART, OTHER):
         give(group).start()
     best = answer[OWN]
-    for group in (OTHER, NEXT, PREVIOUS):
+    for group in (OTHER, X_PART, Y_PART):
         arrival(near.at[group], back_near.at[group]).wait()
         best = jnp.maximum(best, near[group])
     block_of = lax.div(iota((8, 128), 1), PIECE)
@@ -333,31 +379,30 @@
             spaced = jnp.where((iota((8, 128), 0) == t) & (block_of == t), moved[t - source], spaced)
         final[source] = jnp.sum(spaced, axis=0, keepdims=True)
 
-    number = SIDE * z + x
-
-    def spread(step, up):
-        column = lax.rem(x + step, SIDE)
-        return pltpu.make_async_remote_copy(
-            src_ref=final.at[column], dst_ref=returned.at[number], send_sem=back_sent.at[up, step],
-            recv_sem=back_arrive, device_id=(place(column, y, core), plane(z + up)), device_id_type=MESH,
-        )
-
-    spreads = [spread(step, up) for up in (4, 3, 5, 2, 6, 1, 7, 0) for step in (2, 1, 3, 0) if step or up]
+    def spread(source, up):
+        return pltpu.make_async_remote_copy(
+            src_ref=final.at[source], dst_ref=returned.at[numbers[0]], send_sem=back_sent.at[up, source],
+            recv_sem=back_arrive, device_id=(place(*chips[source], core), plane(z + up)), device_id_type=MESH,
+        )
+
+    spreads = [spread(source, up) for up in (4, 3, 5, 2, 6, 1, 7, 0) for source in (3, 1, 2, 0) if source or up]
     for copy in spreads:
         copy.start()
-    pltpu.make_async_copy(final.at[x], returned.at[number], back_arrive).start()
-
-    for group in (OTHER, NEXT, PREVIOUS):
+    pltpu.make_async_copy(final.at[0], returned.at[numbers[0]], back_arrive).start()
+
+    for group in (OTHER, X_PART, Y_PART):
         give(group).wait_send()
 
-    def end_stage(t, carry):
+    for t in range(STAGES):
+        end_ships(t)
         swap(t).wait_send()
-        for source in range(SIDE):
-            for group in (NEXT, PREVIOUS):
-                pass_on(t, source, piece(t, OWN, source), group).wait_send()
-        return carry
-
-    lax.fori_loop(0, STAGES, end_stage, 0)
+        for group in (X_PART, Y_PART):
+            for source in range(SIDE):
+                if source != FAR_SOURCE or t not in DETOURS:
+                    pass_on(t, source, piece(t, OWN, source), group).wait_send()
+            if t in DETOURS:
+                detour(t, group).wait_send()
+                pass_detour(t, group).wait_send()
     for copy in spreads:
         copy.wait_send()
     pltpu.make_async_copy(returned, returned, back_arrive).wait()
@@ -401,6 +446,7 @@
             pltpu.VMEM((SIDE, 1, 128), F32),
             pltpu.VMEM((CLUSTERS, 1, 128), F32),
             pltpu.VMEM((LINES, 128), F32),
+            pltpu.VMEM((2, STAGES, PIECE, WIDTH), BF16),
             dma,
             dma((LOADS,)),
             dma((STAGES, SIDE)),
@@ -414,6 +460,9 @@
             dma((PLANES, SIDE)),
             dma,
             pltpu.SemaphoreType.REGULAR((STAGES,)),
+            dma((2, STAGES)),
+            dma((2, STAGES)),
+            dma((2, STAGES)),
         ],
         compiler_params=pltpu.CompilerParams(
             collective_id=0, has_side_effects=True, vmem_limit_bytes=53 * 2**20

time: 47.3 us -> 45.7 us (0.966); the launches traced: 47.1 us -> 44.8 us
  Pallas kernels: 45.8 us -> 43.5 us
    pallas_call x1, Pallas kernels: 45.8 us -> 43.5 us  [local(): pl.pallas_call(kernel, out_shape=jax.ShapeDtypeStruct((LINES, 128), F32),...]
where the time goes in v5:
time: 45.7 us; the launch traced here: 44.8 us
  Pallas kernels  43.5 us (95%)
  local copies, waits for them, and re-layouts  1.3 us (3%)
    pallas_call x1, Pallas kernels, local(): pl.pallas_call(kernel, out_shape=jax.ShapeDtypeStruct((LINES, 128), F32),...  43.5 us
    unnamed x3, local copies, waits for them, and re-layouts  1.3 us

profile of v5, /device:TPU:1, one launch (start us, length us, event | category | flops | bytes accessed | tf_op | source)
XLA Modules:
  0.0 44.8 jit_solution(7835319224960843820)
XLA Ops:
  0.0 0.0 copy-start
  0.0 0.7 %copy-done = s32[2048]{0:T(1024)S(1)} copy-done((s32[2048]{0:T(1024)S(1)}, s32[2048]{0:T(1024)}, u32[]{:S(2)}) %copy-start) | copy-done | bytes 8216
  0.7 43.5 %shard_map.28 = f32[16,128]{1,0:T(8,128)S(1)} custom-call(s32[16,128]{1,0:T(8,128)S(1)} %bitcast.3, bf16[2048,1024]{1,0:T(8,128)(2,1)} %embeds_ref.1), custom_call_target="tpu_custom_call" | custom-call | flops 8000000000 | bytes 4194304 | tf_op jit(solution)/shard_map/pallas_call | solution.py:429
  44.2 0.6 %copy.4 = f32[2048]{0:T(1024)} copy(f32[2048]{0:T(1024)S(1)} %bitcast.2) | data formatting | bytes 16384
Async XLA Ops:
  0.0 0.7 %copy-start = (s32[2048]{0:T(1024)S(1)}, s32[2048]{0:T(1024)}, u32[]{:S(2)}) copy-start(s32[2048]{0:T(1024)} %param.3) | copy-start | bytes 24580

commit v6 on v5

--- a/solution.py
+++ b/solution.py
@@ -23,8 +23,7 @@
 REGION = STAGES * GROUP
 MEMBERS = 4 * REGION
 LOADS = 8
-DETOURS = (0, 1)
-FAR_SOURCE = 3
+DETOURS = ((0, 3), (1, 3))
 LINES = DOCS // 128
 OWN, OTHER, Y_PART, X_PART = range(4)
 
@@ -89,6 +88,8 @@
     def greet(device):
         pl.semaphore_signal(barrier, inc=1, device_id=device, device_id_type=MESH)
 
+    greet((place(out_x, y, core), plane(z - 1)))
+    greet((place(x, out_y, core + 1 - odd_y), plane(z + 1)))
     for dx in (-1, 0, 1):
         for dy in (-1, 0, 1):
             if dx or dy:
@@ -98,8 +99,6 @@
     greet((sibling, z))
     greet((docs, plane(z + 1)))
     greet((docs, plane(z - 1)))
-    greet((place(out_x, y, core), plane(z - 1)))
-    greet((place(x, out_y, core + 1 - odd_y), plane(z + 1)))
 
     cluster_load.wait()
     clusters = cluster_ref[...]
@@ -189,27 +188,35 @@
         pass_on(t, source, src, X_PART).start()
         pass_on(t, source, src, Y_PART).start()
 
-    def detour(t, group):
-        way = group - Y_PART
-        return pltpu.make_async_remote_copy(
-            src_ref=piece(t, OWN, FAR_SOURCE), dst_ref=detours.at[way, t],
-            send_sem=detour_sent.at[way, t], recv_sem=detour_arrive.at[way, t],
+    def detour(number, group):
+        (t, source), way = DETOURS[number], group - Y_PART
+        return pltpu.make_async_remote_copy(
+            src_ref=piece(t, OWN, source), dst_ref=detours.at[way, number],
+            send_sem=detour_sent.at[way, number], recv_sem=detour_arrive.at[way, number],
             device_id=(to_x, plane(z + 1)) if group == X_PART else (to_y, plane(z - 1)), device_id_type=MESH,
         )
 
-    def pass_detour(t, group):
-        way = group - Y_PART
-        return pltpu.make_async_remote_copy(
-            src_ref=detours.at[way, t], dst_ref=piece(t, group, FAR_SOURCE),
-            send_sem=detour_passed.at[way, t], recv_sem=near_arrive.at[t, FAR_SOURCE, way],
+    def pass_detour(number, group):
+        (t, source), way = DETOURS[number], group - Y_PART
+        return pltpu.make_async_remote_copy(
+            src_ref=detours.at[way, number], dst_ref=piece(t, group, source),
+            send_sem=detour_passed.at[way, number], recv_sem=near_arrive.at[t, source, way],
             device_id=(docs, plane(z - 1) if group == X_PART else plane(z + 1)), device_id_type=MESH,
         )
 
+    def start_detours(t):
+        for number, (stage, source) in enumerate(DETOURS):
+            if stage == t:
+                detour(number, X_PART).start()
+                detour(number, Y_PART).start()
+
     def pass_detours(t):
-        for group in (X_PART, Y_PART):
-            way = group - Y_PART
-            arrival(detours.at[way, t], detour_arrive.at[way, t]).wait()
-            pass_detour(t, group).start()
+        for number, (stage, source) in enumerate(DETOURS):
+            if t == min(stage + 2, STAGES - 1):
+                for group in (X_PART, Y_PART):
+                    way = group - Y_PART
+                    arrival(detours.at[way, number], detour_arrive.at[way, number]).wait()
+                    pass_detour(number, group).start()
 
     def swap(t):
         return pltpu.make_async_remote_copy(
@@ -234,11 +241,9 @@
     def relay(t):
         for source in (1, 2, 3):
             arrival(piece(t, OWN, source), arrive.at[t, source]).wait()
-            if source == FAR_SOURCE and t in DETOURS:
-                detour(t, X_PART).start()
-                detour(t, Y_PART).start()
-            else:
+            if (t, source) not in DETOURS:
                 pass_both(t, source, piece(t, OWN, source))
+        start_detours(t)
         arrival(piece(t, OWN, 0), arrive.at[t, 0]).wait()
         swap(t).start()
 
@@ -333,17 +338,16 @@
         relay(t)
         if t == 1:
             start_ships(3)
-        if t - 1 in DETOURS:
-            pass_detours(t - 1)
-        hear(t)
-        if t + 1 < STAGES:
-            tell(t + 1)
-        if t == 0:
-            everyone, place_in, _ = ranks(list(range(CLUSTERS)))
-            own_rank = jnp.zeros((LINES, 128), F32)
-            for number, mask in enumerate(everyone):
-                own_rank = own_rank + mask * place_in[number * LINES : (number + 1) * LINES]
-            rank_of[...] = own_rank
+        pass_detours(t)
+        if t:
+            hear(t - 1)
+            tell(t)
+
+    everyone, place_in, _ = ranks(list(range(CLUSTERS)))
+    own_rank = jnp.zeros((LINES, 128), F32)
+    for number, mask in enumerate(everyone):
+        own_rank = own_rank + mask * place_in[number * LINES : (number + 1) * LINES]
+    rank_of[...] = own_rank
 
     for t in range(STAGES):
         swap(t).wait_recv()
@@ -379,6 +383,8 @@
             spaced = jnp.where((iota((8, 128), 0) == t) & (block_of == t), moved[t - source], spaced)
         final[source] = jnp.sum(spaced, axis=0, keepdims=True)
 
+    hear(STAGES - 1)
+
     def spread(source, up):
         return pltpu.make_async_remote_copy(
             src_ref=final.at[source], dst_ref=returned.at[numbers[0]], send_sem=back_sent.at[up, source],
@@ -398,11 +404,12 @@
         swap(t).wait_send()
         for group in (X_PART, Y_PART):
             for source in range(SIDE):
-                if source != FAR_SOURCE or t not in DETOURS:
+                if (t, source) not in DETOURS:
                     pass_on(t, source, piece(t, OWN, source), group).wait_send()
-            if t in DETOURS:
-                detour(t, group).wait_send()
-                pass_detour(t, group).wait_send()
+    for number in range(len(DETOURS)):
+        for group in (X_PART, Y_PART):
+            detour(number, group).wait_send()
+            pass_detour(number, group).wait_send()
     for copy in spreads:
         copy.wait_send()
     pltpu.make_async_copy(returned, returned, back_arrive).wait()
@@ -446,7 +453,7 @@
             pltpu.VMEM((SIDE, 1, 128), F32),
             pltpu.VMEM((CLUSTERS, 1, 128), F32),
             pltpu.VMEM((LINES, 128), F32),
-            pltpu.VMEM((2, STAGES, PIECE, WIDTH), BF16),
+            pltpu.VMEM((2, len(DETOURS), PIECE, WIDTH), BF16),
             dma,
             dma((LOADS,)),
             dma((STAGES, SIDE)),
@@ -460,9 +467,9 @@
             dma((PLANES, SIDE)),
             dma,
             pltpu.SemaphoreType.REGULAR((STAGES,)),
-            dma((2, STAGES)),
-            dma((2, STAGES)),
-            dma((2, STAGES)),
+            dma((2, len(DETOURS))),
+            dma((2, len(DETOURS))),
+            dma((2, len(DETOURS))),
         ],
         compiler_params=pltpu.CompilerParams(
             collective_id=0, has_side_effects=True, vmem_limit_bytes=53 * 2**20

time: 45.7 us -> 45.6 us (level)
  no operation moved by 1% of the time
where the time goes in v6:
time: 45.6 us; the launch traced here: 44.7 us
  Pallas kernels  43.4 us (95%)
  local copies, waits for them, and re-layouts  1.3 us (3%)
    pallas_call x1, Pallas kernels, local(): pl.pallas_call(kernel, out_shape=jax.ShapeDtypeStruct((LINES, 128), F32),...  43.4 us
    unnamed x3, local copies, waits for them, and re-layouts  1.3 us

profile of v6, /device:TPU:1, one launch (start us, length us, event | category | flops | bytes accessed | tf_op | source)
XLA Modules:
  0.0 44.7 jit_solution(10746365210733287085)
XLA Ops:
  0.0 0.0 copy-start
  0.0 0.7 %copy-done = s32[2048]{0:T(1024)S(1)} copy-done((s32[2048]{0:T(1024)S(1)}, s32[2048]{0:T(1024)}, u32[]{:S(2)}) %copy-start) | copy-done | bytes 8216
  0.7 43.4 %shard_map.28 = f32[16,128]{1,0:T(8,128)S(1)} custom-call(s32[16,128]{1,0:T(8,128)S(1)} %bitcast.3, bf16[2048,1024]{1,0:T(8,128)(2,1)} %embeds_ref.1), custom_call_target="tpu_custom_call" | custom-call | flops 8000000000 | bytes 4194304 | tf_op jit(solution)/shard_map/pallas_call | solution.py:436
  44.1 0.6 %copy.4 = f32[2048]{0:T(1024)} copy(f32[2048]{0:T(1024)S(1)} %bitcast.2) | data formatting | bytes 16384
Async XLA Ops:
  0.0 0.7 %copy-start = (s32[2048]{0:T(1024)S(1)}, s32[2048]{0:T(1024)}, u32[]{:S(2)}) copy-start(s32[2048]{0:T(1024)} %param.3) | copy-start | bytes 24580

commit v7 on v6

--- a/solution.py
+++ b/solution.py
@@ -334,6 +334,12 @@
         keep(t)
     col_max[...] = jnp.full(col_max.shape, LOWEST, F32)
     answer[...] = jnp.full(answer.shape, LOWEST, F32)
+    everyone, place_in, _ = ranks(list(range(CLUSTERS)))
+    own_rank = jnp.zeros((LINES, 128), F32)
+    for number, mask in enumerate(everyone):
+        own_rank = own_rank + mask * place_in[number * LINES : (number + 1) * LINES]
+    rank_of[...] = own_rank
+
     for t in range(STAGES):
         relay(t)
         if t == 1:
@@ -342,12 +348,6 @@
         if t:
             hear(t - 1)
             tell(t)
-
-    everyone, place_in, _ = ranks(list(range(CLUSTERS)))
-    own_rank = jnp.zeros((LINES, 128), F32)
-    for number, mask in enumerate(everyone):
-        own_rank = own_rank + mask * place_in[number * LINES : (number + 1) * LINES]
-    rank_of[...] = own_rank
 
     for t in range(STAGES):
         swap(t).wait_recv()

time: 45.6 us -> 45.2 us (level); the launches traced: 44.7 us -> 44.8 us
  no operation moved by 1% of the time
where the time goes in v7:
time: 45.2 us; the launch traced here: 44.8 us
  Pallas kernels  43.5 us (96%)
  local copies, waits for them, and re-layouts  1.3 us (3%)
    pallas_call x1, Pallas kernels, local(): pl.pallas_call(kernel, out_shape=jax.ShapeDtypeStruct((LINES, 128), F32),...  43.5 us
    unnamed x3, local copies, waits for them, and re-layouts  1.3 us

profile of v7, /device:TPU:1, one launch (start us, length us, event | category | flops | bytes accessed | tf_op | source)
XLA Modules:
  0.0 44.8 jit_solution(9148676280929578151)
XLA Ops:
  0.0 0.0 copy-start
  0.0 0.7 %copy-done = s32[2048]{0:T(1024)S(1)} copy-done((s32[2048]{0:T(1024)S(1)}, s32[2048]{0:T(1024)}, u32[]{:S(2)}) %copy-start) | copy-done | bytes 8216
  0.7 43.5 %shard_map.28 = f32[16,128]{1,0:T(8,128)S(1)} custom-call(s32[16,128]{1,0:T(8,128)S(1)} %bitcast.3, bf16[2048,1024]{1,0:T(8,128)(2,1)} %embeds_ref.1), custom_call_target="tpu_custom_call" | custom-call | flops 8000000000 | bytes 4194304 | tf_op jit(solution)/shard_map/pallas_call | solution.py:436
  44.2 0.6 %copy.4 = f32[2048]{0:T(1024)} copy(f32[2048]{0:T(1024)S(1)} %bitcast.2) | data formatting | bytes 16384
Async XLA Ops:
  0.0 0.7 %copy-start = (s32[2048]{0:T(1024)S(1)}, s32[2048]{0:T(1024)}, u32[]{:S(2)}) copy-start(s32[2048]{0:T(1024)} %param.3) | copy-start | bytes 24580

commit v8 on v7

--- a/solution.py
+++ b/solution.py
@@ -22,7 +22,7 @@
 GROUP = SIDE * PIECE
 REGION = STAGES * GROUP
 MEMBERS = 4 * REGION
-LOADS = 8
+LOADS = 4
 DETOURS = ((0, 3), (1, 3))
 LINES = DOCS // 128
 OWN, OTHER, Y_PART, X_PART = range(4)

time: 45.2 us -> 45.2 us (level)
  no operation moved by 1% of the time
where the time goes in v8:
time: 45.2 us; the launch traced here: 44.8 us
  Pallas kernels  43.5 us (96%)
  local copies, waits for them, and re-layouts  1.3 us (3%)
    pallas_call x1, Pallas kernels, local(): pl.pallas_call(kernel, out_shape=jax.ShapeDtypeStruct((LINES, 128), F32),...  43.5 us
    unnamed x3, local copies, waits for them, and re-layouts  1.3 us

profile of v8, /device:TPU:1, one launch (start us, length us, event | category | flops | bytes accessed | tf_op | source)
XLA Modules:
  0.0 44.8 jit_solution(16390897243429366052)
XLA Ops:
  0.0 0.0 copy-start
  0.0 0.7 %copy-done = s32[2048]{0:T(1024)S(1)} copy-done((s32[2048]{0:T(1024)S(1)}, s32[2048]{0:T(1024)}, u32[]{:S(2)}) %copy-start) | copy-done | bytes 8216
  0.7 43.5 %shard_map.28 = f32[16,128]{1,0:T(8,128)S(1)} custom-call(s32[16,128]{1,0:T(8,128)S(1)} %bitcast.3, bf16[2048,1024]{1,0:T(8,128)(2,1)} %embeds_ref.1), custom_call_target="tpu_custom_call" | custom-call | flops 8000000000 | bytes 4194304 | tf_op jit(solution)/shard_map/pallas_call | solution.py:436
  44.2 0.6 %copy.4 = f32[2048]{0:T(1024)} copy(f32[2048]{0:T(1024)S(1)} %bitcast.2) | data formatting | bytes 16384
Async XLA Ops:
  0.0 0.7 %copy-start = (s32[2048]{0:T(1024)S(1)}, s32[2048]{0:T(1024)}, u32[]{:S(2)}) copy-start(s32[2048]{0:T(1024)} %param.3) | copy-start | bytes 24580
